TPU v7x, 512 devices: a whole 4x8x8 slice. The times are simulated.
512 devices in a mesh: cell: 32 (over z, x), gene: 16 (over y, core).
Axes of the slice: x: 4, y: 8, z: 8, core: 2. Of those that a mesh axis runs over, the one named last changes fastest.
Arguments:
- block_values: bfloat16 [32, 16, 96, 128, 128], P('cell', 'gene'), may hold values from -6 to 6, as said below
- block_ids: int32 [32, 16, 96], P('cell', 'gene'), may hold values from 0 to 119, as said below
- block_count: int32 [32, 16], P('cell', 'gene'), may hold values from 12 to 96, as said below
- cell_factor: bfloat16 [16384, 128], P('cell'), may hold values from -6 to 6
- gene_factor: bfloat16 [61440, 128], P('gene'), may hold values from -1.796875 to 1.796875
Outputs:
- new_cells: bfloat16 [16384, 128], P('cell')
- new_genes: bfloat16 [61440, 128], P('gene')
Inputs may be any that keep to these rules, and one draw needn't show every extreme that they name: `block_ids`: within one device's list the 96 entries are distinct. Only the first block_count slots of a device's list are live; the values of the other slots are not used. Some device has all 96 slots live. `block_values`: about four entries in ten are zero.
All inputs are finite; a program needn't handle non-finite values.
Results may differ from a plain program's by a relative error of at most 0.012.
Values may be sent and summed in bfloat16 or wider, within the bound.
No kernel may reach another device: no remote copies, remote signals or barrier semaphores. Data moves between devices by JAX's collectives and lax.ppermute only.
A program may use at most 64 MiB of HBM per device.

v0:
```python
import jax
import jax.numpy as jnp
from jax import lax
from jax.sharding import PartitionSpec as P

LAMBDA = 0.5


def solve_right(matrix, gram):
    eye = jnp.eye(gram.shape[0], dtype=jnp.float32)
    lower_factor = jnp.linalg.cholesky(gram + LAMBDA * eye)
    middle = lax.linalg.triangular_solve(
        lower_factor, matrix, left_side=False, lower=True, transpose_a=True
    )
    return lax.linalg.triangular_solve(
        lower_factor, middle, left_side=False, lower=True, transpose_a=False
    )


def body(block_values, block_ids, block_count, cell_factor, gene_factor):
    values = block_values[0, 0]
    ids = block_ids[0, 0]
    count = block_count[0, 0]
    slot_total = ids.shape[0]
    block_size = values.shape[1]
    rank_width = gene_factor.shape[1]
    cell_rows = cell_factor.shape[0]
    gene_rows_dev = gene_factor.shape[0]
    cell_blocks_dev = cell_rows // block_size
    gene_blocks_dev = gene_rows_dev // block_size
    scale = (cell_rows * lax.axis_size("cell")) ** (-0.5)
    cell_tiles = cell_factor.reshape(cell_blocks_dev, block_size, rank_width)
    rows = ids // gene_blocks_dev
    cols = ids % gene_blocks_dev
    cell_blocks = cell_tiles[rows]
    live = jnp.arange(slot_total, dtype=jnp.int32) < count
    keep = live[:, None, None] & (values != 0)

    def residual(gene_tiles):
        gene_blocks = gene_tiles[cols]
        fitted = scale * jnp.einsum(
            "nir,njr->nij", cell_blocks, gene_blocks, preferred_element_type=jnp.float32
        )
        resid = jnp.where(keep, values.astype(jnp.float32) - fitted, 0.0).astype(jnp.bfloat16)
        return (resid, gene_blocks)

    old_tiles = gene_factor.reshape(gene_blocks_dev, block_size, rank_width)
    resid, unused_blocks = residual(old_tiles)
    gene_block_terms = jnp.einsum(
        "nij,nir->njr", resid, cell_blocks, preferred_element_type=jnp.float32
    )
    gene_zero = jnp.zeros((gene_blocks_dev, block_size, rank_width), jnp.float32)
    gene_local = (scale * gene_zero.at[cols].add(gene_block_terms)).reshape(
        gene_rows_dev, rank_width
    )
    gram_local = (
        scale * scale * jnp.dot(cell_factor.T, cell_factor, preferred_element_type=jnp.float32)
    )
    gene_sums, gram_cells = lax.psum((gene_local, gram_local), "cell")
    right_side = gene_sums + jnp.dot(
        gene_factor.astype(jnp.float32), gram_cells, precision=lax.Precision.HIGHEST
    )
    new_genes = solve_right(right_side, gram_cells).astype(jnp.bfloat16)
    gram_genes = lax.psum(
        jnp.dot(new_genes.T, new_genes, preferred_element_type=jnp.float32).astype(jnp.bfloat16),
        "gene",
    ).astype(jnp.float32)
    new_tiles = new_genes.reshape(gene_blocks_dev, block_size, rank_width)
    resid_second, new_blocks = residual(new_tiles)
    cell_block_terms = jnp.einsum(
        "nij,njr->nir", resid_second, new_blocks, preferred_element_type=jnp.float32
    )
    cell_zero = jnp.zeros((cell_blocks_dev, block_size, rank_width), jnp.float32)
    cell_local = cell_zero.at[rows].add(cell_block_terms).reshape(cell_rows, rank_width)
    cell_sums = lax.psum(cell_local, "gene")
    right_cells = cell_sums + scale * jnp.dot(
        cell_factor.astype(jnp.float32), gram_genes, precision=lax.Precision.HIGHEST
    )
    new_cells = (solve_right(right_cells, gram_genes) / scale).astype(jnp.bfloat16)
    return (new_cells, new_genes)


def solution(mesh):
    return jax.shard_map(
        body,
        mesh=mesh,
        in_specs=(
            P("cell", "gene", None, None, None),
            P("cell", "gene", None),
            P("cell", "gene"),
            P("cell", None),
            P("gene", None),
        ),
        out_specs=(P("cell", None), P("gene", None)),
        check_vma=False,
    )
```

profile of v0, /device:TPU:1, one launch (start us, length us, event | category | flops | bytes accessed | tf_op | source)
XLA Modules:
  0.0 452.3 jit_solution(7121882862087395317)
XLA Ops:
  7.2 0.7 fusion.36
  8.6 1.8 convolution_multiply_fusion.2
  10.5 3.7 gather_fusion
  14.1 2.7 gather_fusion.1
  16.8 11.4 %fusion.7 = f32[96,128,128]{2,1,0:T(8,128)} fusion(bf16[96,128,128]{2,1,0:T(8,128)(2,1)} %gather_fusion, bf16[1,1,96,128,128]{4,3,2,1,0:T(8,128)(2,1)} %param.6, pred[96]{0:T(512)(128)(4,1)S(1)} %iota_compare_fusion.2, bf16[96,128,128]{2,1,0:T(8,128)(2,1)} %gather_fusion.1), kind=kOutput, calls=%fused_computation.16 | convolution fusion | flops 819462144 | bytes 15728736 | tf_op jit(solution)/shard_map/nij,nir->njr/dot_general | solution.py:49
  28.5 12.9 %scatter_fusion = f32[30,128,128]{2,1,0:T(8,128)S(1)} fusion(f32[30,128,128]{2,1,0:T(8,128)S(1)} %broadcast_in_dim.11, s32[96]{0:T(128)S(1)} %get-tuple-element.5, f32[96,128,128]{2,1,0:T(8,128)} %fusion.7), kind=kCustom, calls=%fused_computation.3 | custom fusion | flops 1572864 | bytes 18874752 | tf_op jit(solution)/shard_map/scatter-add | solution.py:53
  41.4 1.4 broadcast_multiply_fusion
  42.9 0.2 all-reduce.4.cloned.1.call-start
  43.1 167.0 %all-reduce.6.cloned.1.call-done = (f32[3840,128]{1,0:T(8,128)}, f32[128,128]{1,0:T(8,128)}) async-done(((f32[3840,128]{1,0:T(8,128)}, f32[128,128]{1,0:T(8,128)}), (f32[3840,128]{1,0:T(8,128)}, f32[128,128]{1,0:T(8,128)})) %all-reduce.6.cloned.1.call-update) | async-done | bytes 2031632 | tf_op jit(solution)/shard_map/psum | solution.py:59
  210.1 0.9 select_add_fusion.1
  211.0 0.9 fusion.33
  212.0 11.7 %cholesky.44 = f32[128,128]{1,0:T(8,128)S(1)} custom-call(f32[128,128]{1,0:T(8,128)S(1)} %copy.9), custom_call_target="Cholesky" | custom-call | tf_op jit(solution)/shard_map/jit(cholesky)/cholesky | solution.py:11
  223.7 0.6 compare_reduce_fusion.1
  224.4 0.7 fusion.24
  225.0 9.8 %custom-call.12 = f32[1,128,128]{1,2,0:T(8,128)S(1)} custom-call(f32[1,128,128]{2,1,0:T(8,128)S(1)} %fusion.24), custom_call_target="InvertDiagBlocksLowerTriangular" | custom-call | tf_op jit(solution)/shard_map/triangular_solve | solution.py:12
  234.9 2.5 fusion.4
  237.4 1.8 fusion.31
  239.2 1.7 convolution_convert_fusion
  240.9 0.5 convolution_convert_fusion.1
  241.3 46.8 %psum.31 = bf16[128,128]{1,0:T(8,128)(2,1)S(1)} all-reduce(bf16[128,128]{1,0:T(8,128)(2,1)S(1)} %convolution_convert_fusion.1), channel_id=1, replica_groups=mesh['cell'=32,'gene'=16] {'gene'}, use_global_device_ids=true, to_apply=%region_7.9 | all-reduce | flops 16384 | bytes 65536 | tf_op jit(solution)/shard_map/psum | solution.py:64
  288.4 11.7 %cholesky.55 = f32[128,128]{1,0:T(8,128)S(1)} custom-call(f32[128,128]{1,0:T(8,128)S(1)} %copy.11), custom_call_target="Cholesky" | custom-call | tf_op jit(solution)/shard_map/jit(cholesky)/cholesky | solution.py:11
  300.1 0.6 compare_reduce_fusion
  300.8 2.7 gather_fusion.2
  303.5 11.7 %fusion.5 = f32[96,128,128]{2,1,0:T(8,128)} fusion(bf16[96,128,128]{2,1,0:T(8,128)(2,1)} %gather_fusion.2, bf16[1,1,96,128,128]{4,3,2,1,0:T(8,128)(2,1)} %param.6, pred[96]{0:T(512)(128)(4,1)S(1)} %iota_compare_fusion.2, bf16[96,128,128]{2,1,0:T(8,128)(2,1)} %gather_fusion), kind=kOutput, calls=%fused_computation.15 | convolution fusion | flops 819462144 | bytes 15728736 | tf_op jit(solution)/shard_map/nij,njr->nir/dot_general | solution.py:70
  315.2 12.9 %scatter_fusion.1 = f32[4,128,128]{2,1,0:T(8,128)S(1)} fusion(f32[4,128,128]{2,1,0:T(8,128)S(1)} %broadcast_in_dim.10, s32[96]{0:T(128)S(1)} %get-tuple-element.6, f32[96,128,128]{2,1,0:T(8,128)} %fusion.5), kind=kCustom, calls=%fused_computation.4 | custom fusion | flops 1572864 | bytes 18874752 | tf_op jit(solution)/shard_map/scatter-add | solution.py:74
  328.1 0.7 copy-done.1
  328.9 0.7 fusion.25
  329.5 9.8 %custom-call.13 = f32[1,128,128]{1,2,0:T(8,128)S(1)} custom-call(f32[1,128,128]{2,1,0:T(8,128)S(1)} %fusion.25), custom_call_target="InvertDiagBlocksLowerTriangular" | custom-call | tf_op jit(solution)/shard_map/triangular_solve | solution.py:12
  339.3 103.6 %all-reduce.4.cloned.1.call-done = f32[512,128]{1,0:T(8,128)} async-done(((f32[512,128]{1,0:T(8,128)}), f32[512,128]{1,0:T(8,128)}) %all-reduce.4.cloned.1.call-update) | async-done | bytes 262160 | tf_op jit(solution)/shard_map/psum | solution.py:75
  442.9 1.1 fusion.22
  444.1 0.4 fusion.27
  444.4 1.0 fusion.23
  (22 shorter events, 0.8 us)
Async XLA Ops:
  7.2 7.0 %copy-start = (bf16[3840,128]{1,0:T(8,128)(2,1)S(1)}, bf16[3840,128]{1,0:T(8,128)(2,1)}, u32[]{:S(2)}) copy-start(bf16[3840,128]{1,0:T(8,128)(2,1)} %param.10) | copy-start | bytes 2949124
  7.2 202.9 %all-reduce.6.cloned.1.call-start = ((), (), s32[]{:S(2)}) async-start(), calls=%async_computation.1 | async-start | bytes 4063232 | tf_op jit(solution)/shard_map/psum | solution.py:59
  42.9 400.1 %all-reduce.4.cloned.1.call-start = ((), (), s32[]{:S(2)}) async-start(), calls=%async_computation | async-start | bytes 524288 | tf_op jit(solution)/shard_map/psum | solution.py:75
  240.9 62.6 %copy-start.3 = (bf16[3840,128]{1,0:T(8,128)(2,1)}, bf16[3840,128]{1,0:T(8,128)(2,1)S(1)}, u32[]{:S(2)}) copy-start(bf16[3840,128]{1,0:T(8,128)(2,1)S(1)} %convolution_convert_fusion) | copy-start | bytes 2949124
  315.2 127.7 %copy-start.2 = (bf16[512,128]{1,0:T(8,128)(2,1)S(1)}, bf16[512,128]{1,0:T(8,128)(2,1)}, u32[]{:S(2)}) copy-start(bf16[512,128]{1,0:T(8,128)(2,1)} %param.9) | copy-start | bytes 393220
  328.1 0.7 copy-start.1
Sparse Core Ops, SparseCore 0:
  43.0 167.0 all-reduce.5
  329.0 113.9 all-reduce.3
where the time goes:
time: 453 us; the launch traced here: 452 us
  waiting for transfers between devices  271 us (60%)
  other arithmetic  75.5 us (17%)
  blocking collectives  46.8 us (10%)
  matrix products  34 us (8%)
  between operations  14.9 us (3%)
  local copies, waits for them, and re-layouts  10.3 us (2%)
    psum x1, waiting for transfers between devices, body(): gene_sums, gram_cells = lax.psum((gene_local, gram_local), 'cell')  167 us
    psum x1, waiting for transfers between devices, body(): cell_sums = lax.psum(cell_local, 'gene')  104 us
    psum x1, blocking collectives, body(): lax.psum(jnp.dot(new_genes.T, new_genes, preferred_element_type=jnp.float...  46.8 us
    another operation x6, other arithmetic, solve_right(): lower_factor = jnp.linalg.cholesky(gram + LAMBDA * eye)  24.8 us
    another operation x4, other arithmetic, solve_right(): lax.linalg.triangular_solve(lower_factor, matrix, left_side=False, lower=...  20.9 us
    scatter-add x1, other arithmetic, body(): gene_zero.at[cols].add(gene_block_terms)  12.9 us
    scatter-add x1, other arithmetic, body(): cell_zero.at[rows].add(cell_block_terms).reshape(cell_rows, rank_width)  12.9 us
    dot_general x1, matrix products, body(): jnp.einsum('nij,njr->nir', resid_second, new_blocks, preferred_element_ty...  11.7 us
  transfers between devices with their start and end apart: 2, of which 2 were waited for; matrix products, arithmetic and copies ran while one was open for 2% of the time, Pallas kernels for 0%

commit v1 on v0

v1 whole, which is shorter than its diff:
```python
import functools

import jax
import jax.numpy as jnp
from jax import lax
from jax.experimental import pallas as pl
from jax.experimental.pallas import tpu as pltpu
from jax.sharding import PartitionSpec as P

LAMBDA = 0.5
F32 = jnp.float32
BF16 = jnp.bfloat16
NN = (((1,), (0,)), ((), ()))
NT = (((1,), (1,)), ((), ()))
TN = (((0,), (0,)), ((), ()))
VMEM_LIMIT = 40 * 1024 * 1024


def dot(a, b, dims=NN):
    return lax.dot_general(a, b, dims, preferred_element_type=F32)


def split(value):
    high = value.astype(BF16)
    return high, (value - high.astype(F32)).astype(BF16)


def fill_positions(ids_ref, count_ref, pos_ref):
    slots = ids_ref.shape[0]

    def clear(i, carry):
        pos_ref[i] = slots
        return carry

    lax.fori_loop(0, pos_ref.shape[0], clear, 0, unroll=8)

    def place(k, carry):
        pos_ref[ids_ref[k]] = k
        return carry

    lax.fori_loop(0, count_ref[0], place, 0)


def residual_pair(vals_ref, pos_ref, resid_ref, cells_ref, genes, first, gene_blocks):
    slots, blk, _ = vals_ref.shape
    for c in range(cells_ref.shape[0] // blk):
        rows = pl.ds(c * blk, blk)
        fit = dot(cells_ref[rows, :], genes, NT)
        for h in range(2):
            slot = pos_ref[c * gene_blocks + first + h]
            live = (slot < slots).astype(F32)
            value = vals_ref[jnp.minimum(slot, slots - 1)].astype(F32) * live
            part = value - fit[:, h * blk : (h + 1) * blk]
            resid_ref[rows, h * blk : (h + 1) * blk] = jnp.where(value != 0.0, part, 0.0).astype(BF16)


def first_pass_kernel(
    start, blocks, scale, gene_blocks, ids_ref, count_ref, vals_ref, cell_ref, gene_ref, out_ref, pos_ref, cells_ref, turned_ref, resid_ref
):
    blk = vals_ref.shape[1]
    fill_positions(ids_ref, count_ref, pos_ref)
    scaled = cell_ref[...].astype(F32) * scale
    cells_ref[...] = scaled.astype(BF16)
    turned_ref[...] = scaled.T.astype(BF16)

    def step(p, carry):
        first = start + 2 * p
        genes = gene_ref[pl.ds(pl.multiple_of(first * blk, blk), 2 * blk), :]
        residual_pair(vals_ref, pos_ref, resid_ref, cells_ref, genes, first, gene_blocks)
        terms = dot(turned_ref[...], resid_ref[...]).astype(BF16)
        out_ref[2 * p] = terms[:, :blk]
        out_ref[2 * p + 1] = terms[:, blk:]
        return carry

    lax.fori_loop(0, blocks // 2, step, 0)


def first_pass(start, blocks, scale, gene_blocks, ids, count, values, cells, genes):
    blk = values.shape[1]
    rows, rank = cells.shape
    smem = pl.BlockSpec(memory_space=pltpu.SMEM)
    vmem = pl.BlockSpec(memory_space=pltpu.VMEM)
    return pl.pallas_call(
        functools.partial(first_pass_kernel, start, blocks, scale, gene_blocks),
        out_shape=jax.ShapeDtypeStruct((blocks, rank, blk), BF16),
        in_specs=[smem, smem, vmem, vmem, vmem],
        out_specs=vmem,
        scratch_shapes=[
            pltpu.SMEM((rows // blk * gene_blocks,), jnp.int32),
            pltpu.VMEM((rows, rank), BF16),
            pltpu.VMEM((rank, rows), BF16),
            pltpu.VMEM((rows, 2 * blk), BF16),
        ],
        compiler_params=pltpu.CompilerParams(vmem_limit_bytes=VMEM_LIMIT),
        name="first_pass",
    )(ids, count, values, cells, genes)


def second_pass_kernel(
    start, blocks, scale, gene_blocks, ids_ref, count_ref, vals_ref, cell_ref, new_ref, sum_ref, out_ref, pos_ref, cells_ref, resid_ref, total_ref
):
    blk = vals_ref.shape[1]
    fill_positions(ids_ref, count_ref, pos_ref)
    cells_ref[...] = (cell_ref[...].astype(F32) * scale).astype(BF16)
    total_ref[...] = sum_ref[...].astype(F32)

    def step(p, carry):
        first = start + 2 * p
        genes = new_ref[pl.ds(pl.multiple_of(2 * p * blk, blk), 2 * blk), :]
        residual_pair(vals_ref, pos_ref, resid_ref, cells_ref, genes, first, gene_blocks)
        total_ref[...] += dot(resid_ref[...], genes)
        return carry

    lax.fori_loop(0, blocks // 2, step, 0)
    out_ref[...] = total_ref[...].astype(out_ref.dtype)


def second_pass(start, blocks, scale, gene_blocks, ids, count, values, cells, new, total, kind):
    blk = values.shape[1]
    rows, rank = cells.shape
    smem = pl.BlockSpec(memory_space=pltpu.SMEM)
    vmem = pl.BlockSpec(memory_space=pltpu.VMEM)
    return pl.pallas_call(
        functools.partial(second_pass_kernel, start, blocks, scale, gene_blocks),
        out_shape=jax.ShapeDtypeStruct((rows, rank), kind),
        in_specs=[smem, smem, vmem, vmem, vmem, vmem],
        out_specs=vmem,
        scratch_shapes=[
            pltpu.SMEM((rows // blk * gene_blocks,), jnp.int32),
            pltpu.VMEM((rows, rank), BF16),
            pltpu.VMEM((rows, 2 * blk), BF16),
            pltpu.VMEM((rows, rank), F32),
        ],
        compiler_params=pltpu.CompilerParams(vmem_limit_bytes=VMEM_LIMIT),
        name="second_pass",
    )(ids, count, values, cells, new, total)


def new_genes_kernel(solve_ref, gene_ref, sums_ref, gram_in_ref, new_ref, gram_ref):
    blk = sums_ref.shape[1]
    blocks = sums_ref.shape[0]
    rank = solve_ref.shape[0]
    gram_ref[...] = gram_in_ref[...]

    def step(p, carry):
        rows = pl.ds(pl.multiple_of(2 * p * blk, blk), 2 * blk)
        genes = gene_ref[rows, :]
        sums = jnp.concatenate([sums_ref[2 * p], sums_ref[2 * p + 1]], axis=1)
        turned = (
            dot(solve_ref[:, 0:rank], genes, NT)
            + dot(solve_ref[:, rank : 2 * rank], genes, NT)
            + dot(solve_ref[:, 2 * rank : 3 * rank], sums)
            + dot(solve_ref[:, 3 * rank : 4 * rank], sums)
        )
        low = turned.astype(BF16)
        new = turned.T.astype(BF16)
        new_ref[rows, :] = new
        gram_ref[...] += dot(low, new)
        return carry

    lax.fori_loop(0, blocks // 2, step, 0)


def make_new_genes(solve, genes, sums, gram):
    vmem = pl.BlockSpec(memory_space=pltpu.VMEM)
    rows = sums.shape[0] * sums.shape[1]
    rank = gram.shape[0]
    return pl.pallas_call(
        new_genes_kernel,
        out_shape=(jax.ShapeDtypeStruct((rows, rank), BF16), jax.ShapeDtypeStruct((rank, rank), F32)),
        in_specs=[vmem] * 4,
        out_specs=(vmem, vmem),
        compiler_params=pltpu.CompilerParams(vmem_limit_bytes=VMEM_LIMIT),
        name="new_genes",
    )(solve, genes, sums, gram)


def inverse_kernel(parts_ref, out_ref):
    rank = out_ref.shape[0]
    gram = parts_ref[0].astype(F32)
    for part in range(1, parts_ref.shape[0]):
        gram = gram + parts_ref[part].astype(F32)
    row = lax.broadcasted_iota(jnp.int32, (rank, rank), 0)
    column = lax.broadcasted_iota(jnp.int32, (rank, rank), 1)
    work = gram + jnp.where(row == column, LAMBDA, 0.0)
    for k in range(rank):
        at_row = row[:, 0:1] == k
        at_column = column[0:1, :] == k
        line = work[k : k + 1, :]
        pivot = 1.0 / work[k : k + 1, k : k + 1]
        side = work[:, k : k + 1] - jnp.where(at_row, 1.0, 0.0)
        line = jnp.where(at_column, 1.0, line) * pivot
        kept = jnp.where(at_column, jnp.where(at_row, 1.0, 0.0), work)
        work = kept - side * line
    product = lax.dot_general(gram, work, NN, precision=lax.Precision.HIGHEST, preferred_element_type=F32)
    high, low = split(product)
    out_ref[:, 0:rank] = high.T
    out_ref[:, rank : 2 * rank] = low.T
    high, low = split(work)
    out_ref[:, 2 * rank : 3 * rank] = high
    out_ref[:, 3 * rank : 4 * rank] = low


def inverse(parts):
    vmem = pl.BlockSpec(memory_space=pltpu.VMEM)
    rank = parts.shape[-1]
    return pl.pallas_call(
        inverse_kernel,
        out_shape=jax.ShapeDtypeStruct((rank, 4 * rank), BF16),
        in_specs=[vmem],
        out_specs=vmem,
        compiler_params=pltpu.CompilerParams(vmem_limit_bytes=VMEM_LIMIT),
        name="inverse",
    )(parts)


def new_cells_kernel(scale, solve_ref, cell_ref, sums_ref, out_ref):
    rank = cell_ref.shape[1]
    sums = (sums_ref[...].astype(F32) * (1.0 / scale)).astype(BF16)
    out_ref[...] = (
        dot(cell_ref[...], solve_ref[:, 0:rank], NT)
        + dot(cell_ref[...], solve_ref[:, rank : 2 * rank], NT)
        + dot(sums, solve_ref[:, 2 * rank : 3 * rank], NT)
        + dot(sums, solve_ref[:, 3 * rank : 4 * rank], NT)
    ).astype(BF16)


def make_new_cells(scale, solve, cells, sums):
    vmem = pl.BlockSpec(memory_space=pltpu.VMEM)
    return pl.pallas_call(
        functools.partial(new_cells_kernel, scale),
        out_shape=jax.ShapeDtypeStruct(cells.shape, BF16),
        in_specs=[vmem] * 3,
        out_specs=vmem,
        compiler_params=pltpu.CompilerParams(vmem_limit_bytes=VMEM_LIMIT),
        name="new_cells",
    )(solve, cells, sums)


def exchange(parts, axes):
    return lax.all_to_all(parts, axes, 0, 0, tiled=True)


def spread(part, axes):
    return exchange(jnp.broadcast_to(part[None], (lax.axis_size(axes),) + part.shape), axes)


def body(block_values, block_ids, block_count, cell_factor, gene_factor):
    values = block_values[0, 0]
    ids = block_ids[0, 0]
    count = block_count[0]
    blk = values.shape[1]
    rows, rank = cell_factor.shape
    gene_blocks = gene_factor.shape[0] // blk
    n_cell, n_gene = lax.axis_size("cell"), lax.axis_size("gene")
    scale = (rows * n_cell) ** (-0.5)
    share = rank // n_gene

    scaled = (cell_factor.astype(F32) * scale).astype(BF16)
    mine = lax.dynamic_slice_in_dim(scaled, lax.axis_index("gene") * share, share, 1)
    gram_rows = lax.dot_general(mine, scaled, TN, preferred_element_type=F32).astype(BF16)

    terms = first_pass(0, gene_blocks, scale, gene_blocks, ids, count, values, cell_factor, gene_factor)
    terms = terms.reshape(n_cell, -1, blk)
    height = terms.shape[1]
    message = jnp.concatenate([terms, jnp.broadcast_to(gram_rows[None], (n_cell, share, rank))], axis=1)
    got = exchange(message, "cell").astype(F32).sum(axis=0)
    gram_cells = spread(got[height:], "gene").reshape(1, rank, rank)
    sums = spread(got[:height].astype(BF16), "cell").reshape(gene_blocks, rank, blk)
    solve_genes = inverse(gram_cells)
    new_genes, gram = make_new_genes(solve_genes, gene_factor, sums, jnp.zeros((rank, rank), F32))
    gram_parts = spread(gram.astype(BF16), "gene")
    cell_terms = second_pass(
        0, gene_blocks, scale, gene_blocks, ids, count, values, cell_factor, new_genes, jnp.zeros((rows, rank), BF16), BF16
    )
    got_cells = exchange(cell_terms.reshape(n_gene, -1, rank), "gene").astype(F32).sum(axis=0).astype(BF16)
    cell_sums = spread(got_cells, "gene").reshape(rows, rank)
    solve_cells = inverse(gram_parts)
    new_cells = make_new_cells(scale, solve_cells, cell_factor, cell_sums)
    return new_cells, new_genes


def solution(mesh):
    return jax.shard_map(
        body,
        mesh=mesh,
        in_specs=(
            P("cell", "gene", None, None, None),
            P("cell", "gene", None),
            P("cell", "gene"),
            P("cell", None),
            P("gene", None),
        ),
        out_specs=(P("cell", None), P("gene", None)),
        check_vma=False,
    )
```

time: 453 us -> 179 us (0.40)
  waiting for transfers between devices: 271 us -> 48.5 us
  other arithmetic: 75.5 us -> 1.24 us
  Pallas kernels: 0 us -> 47.9 us
  matrix products: 34 us -> 0.26 us
  starting transfers between devices: 0.26 us -> 28 us
  between operations: 14.9 us -> 1.42 us
  blocking collectives: 46.8 us -> 40.2 us
    psum x2 -> x0, waiting for transfers between devices: 271 us -> none  [the longest x1 167 us: body(): gene_sums, gram_cells = lax.psum((gene_local, gram_local), 'cell')]
    all_to_all x0 -> x5, waiting for transfers between devices: none -> 48.5 us  [exchange(): return lax.all_to_all(parts, axes, 0, 0, tiled=True)]
    pallas_call x0 -> x6, Pallas kernels: none -> 47.9 us  [the longest x2 22.1 us: inverse(): pl.pallas_call(inverse_kernel, out_shape=jax.ShapeDtypeStruct((rank, 4 *...]
    psum x1 -> x0, blocking collectives: 46.8 us -> none  [body(): lax.psum(jnp.dot(new_genes.T, new_genes, preferred_element_type=jnp.float...]
    another operation x10 -> x0, other arithmetic: 45.7 us -> none  [the longest x6 24.8 us: solve_right(): lower_factor = jnp.linalg.cholesky(gram + LAMBDA * eye)]
    all_to_all x0 -> x1, blocking collectives: none -> 40.2 us  [exchange(): return lax.all_to_all(parts, axes, 0, 0, tiled=True)]
    dot_general x6 -> x1, matrix products: 29.1 us -> 0.26 us  [body(): lax.dot_general(mine, scaled, TN, preferred_element_type=F32).astype(BF16)]
    all_to_all x0 -> x5, starting transfers between devices: none -> 28 us  [exchange(): return lax.all_to_all(parts, axes, 0, 0, tiled=True)]
  transfers between devices with their start and end apart: 2 -> 5, of which waited for: 2 -> 4; matrix products, arithmetic and copies ran while one was open for 2% -> 0% of each run, Pallas kernels for 0% -> 12%
where the time goes in v1:
time: 179 us; the launch traced here: 178 us
  waiting for transfers between devices  48.5 us (27%)
  Pallas kernels  47.9 us (27%)
  blocking collectives  40.2 us (22%)
  starting transfers between devices  28 us (16%)
  local copies, waits for them, and re-layouts  10.4 us (6%)
    all_to_all x5, waiting for transfers between devices, exchange(): return lax.all_to_all(parts, axes, 0, 0, tiled=True)  48.5 us
    all_to_all x1, blocking collectives, exchange(): return lax.all_to_all(parts, axes, 0, 0, tiled=True)  40.2 us
    all_to_all x5, starting transfers between devices, exchange(): return lax.all_to_all(parts, axes, 0, 0, tiled=True)  28 us
    pallas_call x2, Pallas kernels, inverse(): pl.pallas_call(inverse_kernel, out_shape=jax.ShapeDtypeStruct((rank, 4 *...  22.1 us
    pallas_call x1, Pallas kernels, make_new_genes(): pl.pallas_call(new_genes_kernel, out_shape=(jax.ShapeDtypeStruct((rows, r...  9.13 us
    pallas_call x1, Pallas kernels, second_pass(): pl.pallas_call(functools.partial(second_pass_kernel, start, blocks, scale...  7.94 us
    pallas_call x1, Pallas kernels, first_pass(): pl.pallas_call(functools.partial(first_pass_kernel, start, blocks, scale,...  7.76 us
    unnamed x18, local copies, waits for them, and re-layouts  7.07 us
  transfers between devices with their start and end apart: 5, of which 4 were waited for; matrix products, arithmetic and copies ran while one was open for 0% of the time, Pallas kernels for 12%

profile of v1, /device:TPU:1, one launch (start us, length us, event | category | flops | bytes accessed | tf_op | source)
XLA Modules:
  0.0 178.0 jit_solution(3621289987447705245)
XLA Ops:
  0.6 0.9 multiply_convert_fusion
  2.2 0.3 convolution_convert_fusion
  2.5 1.9 %copy-done = bf16[1,1,96,128,128]{4,3,2,1,0:T(8,128)(2,1)S(1)} copy-done((bf16[1,1,96,128,128]{4,3,2,1,0:T(8,128)(2,1)S(1)}, bf16[1,1,96,128,128]{4,3,2,1,0:T(8,128)(2,1)}, u32[]{:S(2)}) %copy-start) | copy-done | bytes 3145752
  4.4 1.2 copy-done.2
  5.6 0.9 copy-done.4
  6.5 0.7 copy-done.7
  7.1 7.8 %first_pass.1 = bf16[30,128,128]{2,1,0:T(8,128)(2,1)S(1)} custom-call(s32[96]{0:T(128)S(1)} %bitcast.16, s32[1]{0:T(128)} %bitcast.9.count_ref, bf16[96,128,128]{2,1,0:T(8,128)(2,1)S(1)} %bitcast.11, bf16[512,128]{1,0:T(8,128)(2,1)S(1)} %copy-done.4, bf16[3840,128]{1,0:T(8,128)(2,1)S(1)} %copy-done.2), custom_call_target="tpu_custom_call" | custom-call | tf_op jit(solution)/shard_map/first_pass/pallas_call | solution.py:83
  14.9 0.1 pad_maximum_fusion
  15.1 40.2 %all_to_all.30 = bf16[32,128,128]{2,1,0:T(8,128)(2,1)S(1)} all-to-all(bf16[32,128,128]{2,1,0:T(8,128)(2,1)S(1)} %pad_maximum_fusion), channel_id=1, replica_groups=mesh['cell'=32,'gene'=16] {'cell'}, dimensions={0} | all-to-all | bytes 2097152 | tf_op jit(solution)/shard_map/all_to_all | solution.py:241
  55.3 0.2 convert_reduce_fusion
  55.4 0.6 broadcast_in_dim.15
  56.1 9.9 %all-to-all-start.1 = ((f32[16,8,128]{2,1,0:T(8,128)}), f32[16,8,128]{2,1,0:T(8,128)S(1)}, u32[]{:S(2)}, u32[]{:S(2)}) async-start(f32[16,8,128]{2,1,0:T(8,128)} %broadcast_in_dim.15), calls=%async_computation.1 | async-start | bytes 131072 | tf_op jit(solution)/shard_map/all_to_all | solution.py:241
  65.9 7.8 %all-to-all-done.1 = f32[16,8,128]{2,1,0:T(8,128)S(1)} async-done(((f32[16,8,128]{2,1,0:T(8,128)}), f32[16,8,128]{2,1,0:T(8,128)S(1)}, u32[]{:S(2)}, u32[]{:S(2)}) %all-to-all-start.1) | async-done | bytes 65568 | tf_op jit(solution)/shard_map/all_to_all | solution.py:241
  73.7 1.1 broadcast_in_dim.16
  74.8 5.7 %all-to-all-start.2 = ((bf16[32,120,128]{2,1,0:T(8,128)(2,1)}), bf16[32,120,128]{2,1,0:T(8,128)(2,1)}, u32[]{:S(2)}, u32[]{:S(2)}) async-start(bf16[32,120,128]{2,1,0:T(8,128)(2,1)} %broadcast_in_dim.16), calls=%async_computation.2 | async-start | bytes 1966080 | tf_op jit(solution)/shard_map/all_to_all | solution.py:241
  80.5 11.1 %inverse.2.solve_ref = bf16[128,512]{1,0:T(8,128)(2,1)S(1)} custom-call(f32[1,128,128]{2,1,0:T(8,128)S(1)} %bitcast.15), custom_call_target="tpu_custom_call" | custom-call | tf_op jit(solution)/shard_map/inverse/pallas_call | solution.py:207
  91.6 14.6 %all-to-all-done.2 = bf16[32,120,128]{2,1,0:T(8,128)(2,1)} async-done(((bf16[32,120,128]{2,1,0:T(8,128)(2,1)}), bf16[32,120,128]{2,1,0:T(8,128)(2,1)}, u32[]{:S(2)}, u32[]{:S(2)}) %all-to-all-start.2) | async-done | bytes 983072 | tf_op jit(solution)/shard_map/all_to_all | solution.py:241
  106.2 1.2 copy-done.3
  107.4 9.1 %new_genes.1 = (bf16[3840,128]{1,0:T(8,128)(2,1)}, f32[128,128]{1,0:T(8,128)S(1)}) custom-call(bf16[128,512]{1,0:T(8,128)(2,1)S(1)} %inverse.2.solve_ref, bf16[3840,128]{1,0:T(8,128)(2,1)S(1)} %copy-done.3, bf16[30,128,128]{2,1,0:T(8,128)(2,1)} %bitcast.5.sums_ref, f32[128,128]{1,0:T(8,128)S(1)} %broadcast_in_dim.17.gram_in_ref), custom_call_target="tpu_custom_call" | custom-call | tf_op jit(solution)/shard_map/new_genes/pallas_call | solution.py:168
  116.6 0.0 copy-start.6
  116.6 1.2 copy-done.6
  117.8 7.9 %second_pass.1 = bf16[512,128]{1,0:T(8,128)(2,1)} custom-call(s32[96]{0:T(128)S(1)} %bitcast.17, s32[1]{0:T(128)} %bitcast.10.count_ref, bf16[96,128,128]{2,1,0:T(8,128)(2,1)S(1)} %bitcast.12, bf16[512,128]{1,0:T(8,128)(2,1)S(1)} %copy-done.5, bf16[3840,128]{1,0:T(8,128)(2,1)S(1)} %copy-done.6, bf16[512,128]{1,0:T(8,128)(2,1)S(1)} %broadcast_in_dim.19.sum_ref), custom_call_target="tpu_custom_call" | custom-call | tf_op jit(solution)/shard_map/second_pass/pallas_call | solution.py:123
  125.7 5.4 %all-to-all-start.4 = ((bf16[16,32,128]{2,1,0:T(8,128)(2,1)}), bf16[16,32,128]{2,1,0:T(8,128)(2,1)S(1)}, u32[]{:S(2)}, u32[]{:S(2)}) async-start(bf16[16,32,128]{2,1,0:T(8,128)(2,1)} %bitcast.6), calls=%async_computation.4 | async-start | bytes 262144 | tf_op jit(solution)/shard_map/all_to_all | solution.py:241
  131.2 9.2 %all-to-all-done.4 = bf16[16,32,128]{2,1,0:T(8,128)(2,1)S(1)} async-done(((bf16[16,32,128]{2,1,0:T(8,128)(2,1)}), bf16[16,32,128]{2,1,0:T(8,128)(2,1)S(1)}, u32[]{:S(2)}, u32[]{:S(2)}) %all-to-all-start.4) | async-done | bytes 131104 | tf_op jit(solution)/shard_map/all_to_all | solution.py:241
  140.4 0.9 broadcast_in_dim.18
  141.3 3.5 %all-to-all-start.3 = ((bf16[16,128,128]{2,1,0:T(8,128)(2,1)}), bf16[16,128,128]{2,1,0:T(8,128)(2,1)S(1)}, u32[]{:S(2)}, u32[]{:S(2)}) async-start(bf16[16,128,128]{2,1,0:T(8,128)(2,1)} %broadcast_in_dim.18), calls=%async_computation.3 | async-start | bytes 1048576 | tf_op jit(solution)/shard_map/all_to_all | solution.py:241
  144.8 16.9 %all-to-all-done.3.parts_ref = bf16[16,128,128]{2,1,0:T(8,128)(2,1)S(1)} async-done(((bf16[16,128,128]{2,1,0:T(8,128)(2,1)}), bf16[16,128,128]{2,1,0:T(8,128)(2,1)S(1)}, u32[]{:S(2)}, u32[]{:S(2)}) %all-to-all-start.3) | async-done | bytes 524320 | tf_op jit(solution)/shard_map/all_to_all | solution.py:241
  161.6 0.7 broadcast_in_dim.20
  162.3 3.6 %all-to-all-start.5 = ((bf16[16,32,128]{2,1,0:T(8,128)(2,1)}), bf16[16,32,128]{2,1,0:T(8,128)(2,1)S(1)}, u32[]{:S(2)}, u32[]{:S(2)}) async-start(bf16[16,32,128]{2,1,0:T(8,128)(2,1)} %broadcast_in_dim.20), calls=%async_computation.5 | async-start | bytes 262144 | tf_op jit(solution)/shard_map/all_to_all | solution.py:241
  165.9 11.1 %inverse.3.solve_ref = bf16[128,512]{1,0:T(8,128)(2,1)S(1)} custom-call(bf16[16,128,128]{2,1,0:T(8,128)(2,1)S(1)} %all-to-all-done.3.parts_ref), custom_call_target="tpu_custom_call" | custom-call | tf_op jit(solution)/shard_map/inverse/pallas_call | solution.py:207
  177.0 0.0 all-to-all-done.5
  177.0 1.0 new_cells.1
  (18 shorter events, 0.1 us)
Async XLA Ops:
  2.5 1.9 %copy-start = (bf16[1,1,96,128,128]{4,3,2,1,0:T(8,128)(2,1)S(1)}, bf16[1,1,96,128,128]{4,3,2,1,0:T(8,128)(2,1)}, u32[]{:S(2)}) copy-start(bf16[1,1,96,128,128]{4,3,2,1,0:T(8,128)(2,1)} %param.5) | copy-start | bytes 9437188
  4.4 1.2 copy-start.2
  5.6 0.9 copy-start.4
  6.5 0.7 copy-start.7
  56.1 17.7 %all-to-all-start.1 = ((f32[16,8,128]{2,1,0:T(8,128)}), f32[16,8,128]{2,1,0:T(8,128)S(1)}, u32[]{:S(2)}, u32[]{:S(2)}) async-start(f32[16,8,128]{2,1,0:T(8,128)} %broadcast_in_dim.15), calls=%async_computation.1 | async-start | bytes 131072 | tf_op jit(solution)/shard_map/all_to_all | solution.py:241
  73.7 42.8 %copy-start.5 = (bf16[512,128]{1,0:T(8,128)(2,1)S(1)}, bf16[512,128]{1,0:T(8,128)(2,1)}, u32[]{:S(2)}) copy-start(bf16[512,128]{1,0:T(8,128)(2,1)} %cell_ref.5) | copy-start | bytes 393220
  73.7 42.8 %copy-start.8 = (s32[1,1,96]{2,1,0:T(1,128)S(1)}, s32[1,1,96]{2,1,0:T(1,128)}, u32[]{:S(2)}) copy-start(s32[1,1,96]{2,1,0:T(1,128)} %param.6) | copy-start | bytes 1156
  74.8 41.8 %copy-start.1 = (bf16[1,1,96,128,128]{4,3,2,1,0:T(8,128)(2,1)S(1)}, bf16[1,1,96,128,128]{4,3,2,1,0:T(8,128)(2,1)}, u32[]{:S(2)}) copy-start(bf16[1,1,96,128,128]{4,3,2,1,0:T(8,128)(2,1)} %param.5) | copy-start | bytes 9437188
  74.8 31.4 %all-to-all-start.2 = ((bf16[32,120,128]{2,1,0:T(8,128)(2,1)}), bf16[32,120,128]{2,1,0:T(8,128)(2,1)}, u32[]{:S(2)}, u32[]{:S(2)}) async-start(bf16[32,120,128]{2,1,0:T(8,128)(2,1)} %broadcast_in_dim.16), calls=%async_computation.2 | async-start | bytes 1966080 | tf_op jit(solution)/shard_map/all_to_all | solution.py:241
  106.2 1.2 copy-start.3
  116.6 1.2 copy-start.6
  125.7 14.7 %all-to-all-start.4 = ((bf16[16,32,128]{2,1,0:T(8,128)(2,1)}), bf16[16,32,128]{2,1,0:T(8,128)(2,1)S(1)}, u32[]{:S(2)}, u32[]{:S(2)}) async-start(bf16[16,32,128]{2,1,0:T(8,128)(2,1)} %bitcast.6), calls=%async_computation.4 | async-start | bytes 262144 | tf_op jit(solution)/shard_map/all_to_all | solution.py:241
  141.3 20.4 %all-to-all-start.3 = ((bf16[16,128,128]{2,1,0:T(8,128)(2,1)}), bf16[16,128,128]{2,1,0:T(8,128)(2,1)S(1)}, u32[]{:S(2)}, u32[]{:S(2)}) async-start(bf16[16,128,128]{2,1,0:T(8,128)(2,1)} %broadcast_in_dim.18), calls=%async_computation.3 | async-start | bytes 1048576 | tf_op jit(solution)/shard_map/all_to_all | solution.py:241
  162.3 14.7 %all-to-all-start.5 = ((bf16[16,32,128]{2,1,0:T(8,128)(2,1)}), bf16[16,32,128]{2,1,0:T(8,128)(2,1)S(1)}, u32[]{:S(2)}, u32[]{:S(2)}) async-start(bf16[16,32,128]{2,1,0:T(8,128)(2,1)} %broadcast_in_dim.20), calls=%async_computation.5 | async-start | bytes 262144 | tf_op jit(solution)/shard_map/all_to_all | solution.py:241

commit v2 on v0

v2 whole, which is shorter than its diff:
```python
import functools

import jax
import jax.numpy as jnp
from jax import lax
from jax.experimental import pallas as pl
from jax.experimental.pallas import tpu as pltpu
from jax.sharding import PartitionSpec as P

LAMBDA = 0.5
F32 = jnp.float32
BF16 = jnp.bfloat16
NN = (((1,), (0,)), ((), ()))
NT = (((1,), (1,)), ((), ()))
PARAMS = pltpu.CompilerParams(vmem_limit_bytes=48 * 1024 * 1024)
SMEM = pl.BlockSpec(memory_space=pltpu.SMEM)
VMEM = pl.BlockSpec(memory_space=pltpu.VMEM)
HBM = pl.BlockSpec(memory_space=pltpu.HBM)
GROUP = 15
PIECES = 4


def dot(a, b, dims=NN):
    return lax.dot_general(a, b, dims, preferred_element_type=F32)


def exact_dot(a, b):
    return lax.dot_general(a, b, NN, precision=lax.Precision.HIGHEST, preferred_element_type=F32)


def split(value):
    high = value.astype(BF16)
    return high, (value - high.astype(F32)).astype(BF16)


def two_terms(value):
    high = value.astype(BF16).astype(F32)
    return jnp.concatenate([high, value - high], axis=0).astype(BF16)


def start_loads(sem, pairs):
    copies = []
    source, target = pairs[0]
    step = source.shape[0] // PIECES
    for i in range(PIECES):
        part = pl.ds(i * step, step)
        copies.append(pltpu.make_async_copy(source.at[part], target.at[part], sem.at[i]))
    for i, (source, target) in enumerate(pairs[1:]):
        copies.append(pltpu.make_async_copy(source, target, sem.at[PIECES + i]))
    for copy in reversed(copies):
        copy.start()
    return copies[:PIECES], copies[PIECES:]


def fill_positions(ids_ref, count_ref, pos_ref):
    slots = ids_ref.shape[0]
    for i in range(pos_ref.shape[0]):
        pos_ref[i] = slots
    count = count_ref[0]
    for k in range(slots):
        pos_ref[ids_ref[k]] = jnp.where(k < count, k, slots)


def residual_pair(vals_ref, pos_ref, resid_ref, cells_ref, genes, first, gene_blocks, at):
    slots, blk, _ = vals_ref.shape
    for c in range(cells_ref.shape[0] // blk):
        rows = pl.ds(c * blk, blk)
        fit = dot(cells_ref[rows, :], genes, NT)
        for h in range(2):
            slot = pos_ref[c * gene_blocks + first + h]
            live = (slot < slots).astype(F32)
            value = vals_ref[jnp.minimum(slot, slots - 1)].astype(F32) * live
            part = value - fit[:, h * blk : (h + 1) * blk]
            to = pl.ds((at + h) * blk, blk)
            resid_ref[rows, to] = jnp.where(value != 0.0, part, 0.0).astype(BF16)


def first_pass_kernel(
    scale, gene_blocks, ids_ref, count_ref, vals_hbm, cell_hbm, gene_hbm, out_ref, sem, pos_ref, vals_ref, cell_ref, gene_ref, turned_ref, resid_ref, flat_ref
):
    blk = vals_ref.shape[1]
    owners, height, _ = out_ref.shape
    share = gene_blocks * blk // owners
    values, others = start_loads(sem, [(vals_hbm, vals_ref), (gene_hbm, gene_ref), (cell_hbm, cell_ref)])
    fill_positions(ids_ref, count_ref, pos_ref)
    others[1].wait()
    scaled = cell_ref[...].astype(F32) * scale
    turned_ref[...] = scaled.T.astype(BF16)
    cell_ref[...] = scaled.astype(BF16)
    gram = dot(turned_ref[...], cell_ref[...])
    rows = (height - share) // 2
    for owner in range(owners):
        out_ref[owner, share:, :] = two_terms(gram[owner * rows : (owner + 1) * rows, :])
    others[0].wait()
    for copy in values:
        copy.wait()

    def step(p, carry):
        for u in range(GROUP):
            first = 2 * (p * GROUP + u)
            genes = gene_ref[pl.ds(pl.multiple_of(first * blk, blk), 2 * blk), :]
            residual_pair(vals_ref, pos_ref, resid_ref, cell_ref, genes, first, gene_blocks, 2 * u)
        terms = dot(turned_ref[...], resid_ref[...]).astype(BF16)
        for u in range(2 * GROUP):
            to = pl.ds(pl.multiple_of((2 * p * GROUP + u) * blk, blk), blk)
            flat_ref[to, :] = terms[:, u * blk : (u + 1) * blk]
        return carry

    lax.fori_loop(0, gene_blocks // (2 * GROUP), step, 0)
    for owner in range(owners):
        out_ref[owner, :share, :] = flat_ref[owner * share : (owner + 1) * share, :]


def first_pass(scale, owners, ids, count, values, cells, genes):
    slots, blk, _ = values.shape
    rows, rank = cells.shape
    gene_blocks = genes.shape[0] // blk
    height = genes.shape[0] // owners + 2 * (rank // owners)
    return pl.pallas_call(
        functools.partial(first_pass_kernel, scale, gene_blocks),
        out_shape=jax.ShapeDtypeStruct((owners, height, blk), BF16),
        in_specs=[SMEM, SMEM, HBM, HBM, HBM],
        out_specs=VMEM,
        scratch_shapes=[
            pltpu.SemaphoreType.DMA((PIECES + 2,)),
            pltpu.SMEM((rows // blk * gene_blocks,), jnp.int32),
            pltpu.VMEM(values.shape, BF16),
            pltpu.VMEM(cells.shape, BF16),
            pltpu.VMEM(genes.shape, BF16),
            pltpu.VMEM((rank, rows), BF16),
            pltpu.VMEM((rows, 2 * GROUP * blk), BF16),
            pltpu.VMEM(genes.shape, BF16),
        ],
        compiler_params=pltpu.CompilerParams(vmem_limit_bytes=63 * 1024 * 1024),
        name="first_pass",
    )(ids, count, values, cells, genes)


def add_up_kernel(share, parts_ref, out_ref):
    parts, height, _ = parts_ref.shape
    step = share // 4 if share % 32 == 0 else share // 5
    low = 0
    while low < share:
        rows = pl.ds(low, step)
        total = parts_ref[0, rows, :].astype(F32)
        for i in range(1, parts):
            total = total + parts_ref[i, rows, :].astype(F32)
        total = total.astype(BF16)
        for i in range(out_ref.shape[0]):
            out_ref[i, rows, :] = total
        low += step
    rows = pl.ds(share, height - share)
    total = parts_ref[0, rows, :].astype(F32)
    for i in range(1, parts):
        total = total + parts_ref[i, rows, :].astype(F32)
    half = (height - share) // 2
    gram = two_terms(total[:half, :] + total[half:, :])
    for i in range(out_ref.shape[0]):
        out_ref[i, rows, :] = gram


def add_up(share, parts):
    return pl.pallas_call(
        functools.partial(add_up_kernel, share),
        out_shape=jax.ShapeDtypeStruct(parts.shape, BF16),
        in_specs=[VMEM],
        out_specs=VMEM,
        compiler_params=PARAMS,
        name="add_up",
    )(parts)


def eliminate(work, row, column):
    for k in range(work.shape[0]):
        at_row = row[:, 0:1] == k
        at_column = column[0:1, :] == k
        line = work[k : k + 1, :]
        pivot = 1.0 / work[k : k + 1, k : k + 1]
        side = work[:, k : k + 1] - jnp.where(at_row, 1.0, 0.0)
        line = jnp.where(at_column, 1.0, line) * pivot
        kept = jnp.where(at_column, jnp.where(at_row, 1.0, 0.0), work)
        work = kept - side * line
    return work


def solve_into(solve_ref, inverse_ref, gram):
    rank = gram.shape[0]
    row = lax.broadcasted_iota(jnp.int32, (rank, rank), 0)
    column = lax.broadcasted_iota(jnp.int32, (rank, rank), 1)
    diagonal = row == column
    eye = jnp.where(diagonal, 1.0, 0.0)
    matrix = gram + LAMBDA * eye
    along = jnp.where(diagonal, matrix, 0.0)
    down = 1.0 / jnp.sum(along, axis=1, keepdims=True)
    across = 1.0 / jnp.sum(along, axis=0, keepdims=True)
    guess = (eye + (eye - matrix * across)) * down
    for turn in range(3):
        rest = eye - exact_dot(matrix, guess)
        if turn == 2:
            size = jnp.sum(rest * rest)
        guess = guess + dot(guess.astype(BF16), rest.astype(BF16))
    inverse_ref[...] = guess

    @pl.when(jnp.logical_not(size < 1e-6))
    def _():
        inverse_ref[...] = eliminate(matrix, row, column)

    inverse = inverse_ref[...]
    high, low = split(exact_dot(inverse, gram))
    solve_ref[:, 0:rank] = high
    solve_ref[:, rank : 2 * rank] = low
    high, low = split(inverse)
    solve_ref[:, 2 * rank : 3 * rank] = high
    solve_ref[:, 3 * rank : 4 * rank] = low


def second_pass_kernel(
    scale,
    share,
    ids_ref,
    count_ref,
    vals_hbm,
    cell_hbm,
    gene_hbm,
    sums_ref,
    new_hbm,
    out_ref,
    sem,
    out_sem,
    pos_ref,
    vals_ref,
    cell_ref,
    gene_ref,
    flat_ref,
    solve_ref,
    gram_ref,
    new_ref,
    turned_ref,
    resid_ref,
    total_ref,
):
    blk = vals_ref.shape[1]
    rank = cell_ref.shape[1]
    gene_blocks = gene_ref.shape[0] // blk
    senders, height, _ = sums_ref.shape
    values, others = start_loads(sem, [(vals_hbm, vals_ref), (gene_hbm, gene_ref), (cell_hbm, cell_ref)])
    fill_positions(ids_ref, count_ref, pos_ref)
    half = (height - share) // 2
    for i in range(senders):
        flat_ref[i * share : (i + 1) * share, :] = sums_ref[i, :share, :]
        gram = sums_ref[i, share:, :].astype(F32)
        gram_ref[i * half : (i + 1) * half, :] = gram[:half, :] + gram[half:, :]
    solve_into(solve_ref, total_ref.at[:rank, :], gram_ref[...])
    for copy in others + values:
        copy.wait()
    cell_ref[...] = (cell_ref[...].astype(F32) * scale).astype(BF16)
    total_ref[...] = jnp.zeros_like(total_ref)
    width = 2 * GROUP * blk
    steps = gene_blocks // (2 * GROUP)

    def store(p):
        rows = pl.ds(pl.multiple_of(p * width, width), width)
        return pltpu.make_async_copy(new_ref.at[rows], new_hbm.at[rows], out_sem.at[p])

    def step(p, carry):
        for u in range(GROUP):
            first = 2 * (p * GROUP + u)
            base = pl.multiple_of(first * blk, 2 * blk)
            old = gene_ref[pl.ds(base, 2 * blk), :]
            sums = jnp.concatenate([flat_ref[pl.ds(base, blk), :], flat_ref[pl.ds(base + blk, blk), :]], axis=1)
            turned = (
                dot(solve_ref[:, 0:rank], old, NT)
                + dot(solve_ref[:, rank : 2 * rank], old, NT)
                + dot(solve_ref[:, 2 * rank : 4 * rank], jnp.concatenate([sums, sums], axis=0))
            )
            genes = turned.T.astype(BF16)
            turned_ref[:, pl.ds(base, 2 * blk)] = turned.astype(BF16)
            new_ref[pl.ds(base, 2 * blk), :] = genes
            residual_pair(vals_ref, pos_ref, resid_ref, cell_ref, genes, first, gene_blocks, 2 * u)
        total_ref[...] += dot(resid_ref[...], new_ref[pl.ds(pl.multiple_of(p * width, width), width), :])
        store(p).start()
        return carry

    lax.fori_loop(0, steps, step, 0)
    gram = dot(turned_ref[...], new_ref[...])
    owners, out_height, _ = out_ref.shape
    count = total_ref.shape[0] // owners
    half = (out_height - count) // 2
    for i in range(owners):
        out_ref[i, :count, :] = total_ref[i * count : (i + 1) * count, :].astype(BF16)
        out_ref[i, count:, :] = two_terms(gram[i * half : (i + 1) * half, :])

    def finish(p, carry):
        store(p).wait()
        return carry

    lax.fori_loop(0, steps, finish, 0)


def second_pass(scale, share, owners, ids, count, values, cells, genes, sums):
    slots, blk, _ = values.shape
    rows, rank = cells.shape
    gene_blocks = genes.shape[0] // blk
    height = rows // owners + 2 * (rank // owners)
    return pl.pallas_call(
        functools.partial(second_pass_kernel, scale, share),
        out_shape=(jax.ShapeDtypeStruct(genes.shape, BF16), jax.ShapeDtypeStruct((owners, height, rank), BF16)),
        in_specs=[SMEM, SMEM, HBM, HBM, HBM, VMEM],
        out_specs=(HBM, VMEM),
        scratch_shapes=[
            pltpu.SemaphoreType.DMA((PIECES + 2,)),
            pltpu.SemaphoreType.DMA((gene_blocks // (2 * GROUP),)),
            pltpu.SMEM((rows // blk * gene_blocks,), jnp.int32),
            pltpu.VMEM(values.shape, BF16),
            pltpu.VMEM(cells.shape, BF16),
            pltpu.VMEM(genes.shape, BF16),
            pltpu.VMEM(genes.shape, BF16),
            pltpu.VMEM((rank, 4 * rank), BF16),
            pltpu.VMEM((rank, rank), F32),
            pltpu.VMEM(genes.shape, BF16),
            pltpu.VMEM((rank, genes.shape[0]), BF16),
            pltpu.VMEM((rows, 2 * GROUP * blk), BF16),
            pltpu.VMEM((rows, rank), F32),
        ],
        compiler_params=PARAMS,
        name="second_pass",
    )(ids, count, values, cells, genes, sums)


def new_cells_kernel(scale, share, cell_ref, sums_ref, out_ref, solve_ref, gram_ref, inverse_ref):
    rank = cell_ref.shape[1]
    senders, height, _ = sums_ref.shape
    half = (height - share) // 2
    for i in range(senders):
        gram = sums_ref[i, share:, :].astype(F32)
        gram_ref[i * half : (i + 1) * half, :] = gram[:half, :] + gram[half:, :]
    solve_into(solve_ref, inverse_ref, gram_ref[...])
    sums = (sums_ref[:, :share, :].reshape(senders * share, rank).astype(F32) * (1.0 / scale)).astype(BF16)
    out_ref[...] = (
        dot(cell_ref[...], solve_ref[:, 0:rank], NT)
        + dot(cell_ref[...], solve_ref[:, rank : 2 * rank], NT)
        + dot(sums, solve_ref[:, 2 * rank : 3 * rank], NT)
        + dot(sums, solve_ref[:, 3 * rank : 4 * rank], NT)
    ).astype(BF16)


def make_new_cells(scale, share, cells, sums):
    rank = cells.shape[1]
    return pl.pallas_call(
        functools.partial(new_cells_kernel, scale, share),
        out_shape=jax.ShapeDtypeStruct(cells.shape, BF16),
        in_specs=[VMEM] * 2,
        out_specs=VMEM,
        scratch_shapes=[
            pltpu.VMEM((rank, 4 * rank), BF16),
            pltpu.VMEM((rank, rank), F32),
            pltpu.VMEM((rank, rank), F32),
        ],
        compiler_params=PARAMS,
        name="new_cells",
    )(cells, sums)


def exchange(parts, axes):
    return lax.all_to_all(parts, axes, 0, 0, tiled=True)


def body(block_values, block_ids, block_count, cell_factor, gene_factor):
    values = block_values[0, 0]
    ids = block_ids[0, 0]
    count = block_count[0]
    rows = cell_factor.shape[0]
    n_cell, n_gene = lax.axis_size("cell"), lax.axis_size("gene")
    scale = (rows * n_cell) ** (-0.5)
    gene_share = gene_factor.shape[0] // n_cell
    cell_share = rows // n_gene

    terms = first_pass(scale, n_cell, ids, count, values, cell_factor, gene_factor)
    sums = exchange(add_up(gene_share, exchange(terms, "cell")), "cell")
    new_genes, cell_terms = second_pass(scale, gene_share, n_gene, ids, count, values, cell_factor, gene_factor, sums)
    cell_sums = exchange(add_up(cell_share, exchange(cell_terms, "gene")), "gene")
    new_cells = make_new_cells(scale, cell_share, cell_factor, cell_sums)
    return new_cells, new_genes


def solution(mesh):
    return jax.shard_map(
        body,
        mesh=mesh,
        in_specs=(
            P("cell", "gene", None, None, None),
            P("cell", "gene", None),
            P("cell", "gene"),
            P("cell", None),
            P("gene", None),
        ),
        out_specs=(P("cell", None), P("gene", None)),
        check_vma=False,
    )
```

time: 453 us -> 148 us (0.33)
  waiting for transfers between devices: 271 us -> 0 us
  other arithmetic: 75.5 us -> 0 us
  blocking collectives: 46.8 us -> 106 us
  Pallas kernels: 0 us -> 40.9 us
  matrix products: 34 us -> 0 us
  between operations: 14.9 us -> 1.35 us
  local copies, waits for them, and re-layouts: 10.3 us -> 0.03 us
    psum x2 -> x0, waiting for transfers between devices: 271 us -> none  [the longest x1 167 us: body(): gene_sums, gram_cells = lax.psum((gene_local, gram_local), 'cell')]
    all_to_all x0 -> x4, blocking collectives: none -> 106 us  [exchange(): return lax.all_to_all(parts, axes, 0, 0, tiled=True)]
    psum x1 -> x0, blocking collectives: 46.8 us -> none  [body(): lax.psum(jnp.dot(new_genes.T, new_genes, preferred_element_type=jnp.float...]
    another operation x10 -> x0, other arithmetic: 45.7 us -> none  [the longest x6 24.8 us: solve_right(): lower_factor = jnp.linalg.cholesky(gram + LAMBDA * eye)]
    pallas_call x0 -> x5, Pallas kernels: none -> 40.9 us  [the longest x1 21.2 us: second_pass(): pl.pallas_call(functools.partial(second_pass_kernel, scale, share), out_s...]
    dot_general x6 -> x0, matrix products: 29.1 us -> none  [the longest x1 11.7 us: body(): jnp.einsum('nij,njr->nir', resid_second, new_blocks, preferred_element_ty...]
    scatter-add x2 -> x0, other arithmetic: 25.8 us -> none  [the longest x1 12.9 us: body(): gene_zero.at[cols].add(gene_block_terms)]
    gather x3 -> x0, local copies, waits for them, and re-layouts: 9.01 us -> none  [the longest x2 5.36 us: residual(): gene_blocks = gene_tiles[cols]]
  transfers between devices with their start and end apart: 2 -> 0, of which waited for: 2 -> 0; matrix products, arithmetic and copies ran while one was open for 2% -> 0% of each run, Pallas kernels for 0% -> 0%
where the time goes in v2:
time: 148 us
  blocking collectives  106 us (72%)
  Pallas kernels  40.9 us (28%)
    all_to_all x4, blocking collectives, exchange(): return lax.all_to_all(parts, axes, 0, 0, tiled=True)  106 us
    pallas_call x1, Pallas kernels, second_pass(): pl.pallas_call(functools.partial(second_pass_kernel, scale, share), out_s...  21.2 us
    pallas_call x1, Pallas kernels, make_new_cells(): pl.pallas_call(functools.partial(new_cells_kernel, scale, share), out_sha...  13.2 us
    pallas_call x1, Pallas kernels, first_pass(): pl.pallas_call(functools.partial(first_pass_kernel, scale, gene_blocks),...  6.22 us

profile of v2, /device:TPU:1, one launch (start us, length us, event | category | flops | bytes accessed | tf_op | source)
XLA Modules:
  0.0 147.8 jit_solution(3304475855543826287)
XLA Ops:
  1.3 6.2 %first_pass.1 = bf16[32,128,128]{2,1,0:T(8,128)(2,1)} custom-call(s32[96]{0:T(128)} %bitcast.7, s32[1]{0:T(128)} %bitcast.3.count_ref, bf16[96,128,128]{2,1,0:T(8,128)(2,1)} %bitcast.5, bf16[512,128]{1,0:T(8,128)(2,1)} %cell_ref.1, bf16[3840,128]{1,0:T(8,128)(2,1)} %gene_hbm.3), custom_call_target="tpu_custom_call" | custom-call | tf_op jit(solution)/shard_map/first_pass/pallas_call | solution.py:119
  7.5 0.0 copy-start
  7.5 0.0 copy-start.1
  7.5 0.0 copy-start.2
  7.5 0.0 copy-start.3
  7.6 40.2 %all_to_all.20.parts_ref = bf16[32,128,128]{2,1,0:T(8,128)(2,1)S(1)} all-to-all(bf16[32,128,128]{2,1,0:T(8,128)(2,1)} %first_pass.1), channel_id=1, replica_groups=mesh['cell'=32,'gene'=16] {'cell'}, dimensions={0} | all-to-all | bytes 2097152 | tf_op jit(solution)/shard_map/all_to_all | solution.py:365
  47.8 0.2 add_up.2
  48.0 31.4 %all_to_all.21.sums_ref = bf16[32,128,128]{2,1,0:T(8,128)(2,1)S(1)} all-to-all(bf16[32,128,128]{2,1,0:T(8,128)(2,1)S(1)} %add_up.2), channel_id=1, replica_groups=mesh['cell'=32,'gene'=16] {'cell'}, dimensions={0} | all-to-all | bytes 2097152 | tf_op jit(solution)/shard_map/all_to_all | solution.py:365
  79.5 0.0 copy-done
  79.5 0.0 copy-done.1
  79.5 0.0 copy-done.2
  79.5 0.0 copy-done.3
  79.5 21.2 %second_pass.1 = (bf16[3840,128]{1,0:T(8,128)(2,1)}, bf16[16,48,128]{2,1,0:T(8,128)(2,1)S(1)}) custom-call(s32[96]{0:T(128)S(1)} %bitcast.8, s32[1]{0:T(128)} %bitcast.4.count_ref, bf16[96,128,128]{2,1,0:T(8,128)(2,1)S(1)} %bitcast.6, bf16[512,128]{1,0:T(8,128)(2,1)S(1)} %copy-done.2, bf16[3840,128]{1,0:T(8,128)(2,1)S(1)} %copy-done.1, ...), custom_call_target="tpu_custom_call" | custom-call | tf_op jit(solution)/shard_map/second_pass/pallas_call | solution.py:305
  100.7 20.9 %all_to_all.22.parts_ref = bf16[16,48,128]{2,1,0:T(8,128)(2,1)S(1)} all-to-all(bf16[16,48,128]{2,1,0:T(8,128)(2,1)S(1)} %get-tuple-element.4), channel_id=1, replica_groups=mesh['cell'=32,'gene'=16] {'gene'}, dimensions={0} | all-to-all | bytes 393216 | tf_op jit(solution)/shard_map/all_to_all | solution.py:365
  121.7 13.0 %all_to_all.23.sums_ref = bf16[16,48,128]{2,1,0:T(8,128)(2,1)S(1)} all-to-all(bf16[16,48,128]{2,1,0:T(8,128)(2,1)S(1)} %add_up.3), channel_id=1, replica_groups=mesh['cell'=32,'gene'=16] {'gene'}, dimensions={0} | all-to-all | bytes 393216 | tf_op jit(solution)/shard_map/all_to_all | solution.py:365
  134.6 13.2 %new_cells.1 = bf16[512,128]{1,0:T(8,128)(2,1)} custom-call(bf16[512,128]{1,0:T(8,128)(2,1)S(1)} %copy-done.2, bf16[16,48,128]{2,1,0:T(8,128)(2,1)S(1)} %all_to_all.23.sums_ref), custom_call_target="tpu_custom_call" | custom-call | tf_op jit(solution)/shard_map/new_cells/pallas_call | solution.py:349
  (1 shorter events, 0.0 us)
Async XLA Ops:
  7.5 71.9 %copy-start = (bf16[1,1,96,128,128]{4,3,2,1,0:T(8,128)(2,1)S(1)}, bf16[1,1,96,128,128]{4,3,2,1,0:T(8,128)(2,1)}, u32[]{:S(2)}) copy-start(bf16[1,1,96,128,128]{4,3,2,1,0:T(8,128)(2,1)} %param.5) | copy-start | bytes 9437188
  7.5 71.9 %copy-start.1 = (bf16[3840,128]{1,0:T(8,128)(2,1)S(1)}, bf16[3840,128]{1,0:T(8,128)(2,1)}, u32[]{:S(2)}) copy-start(bf16[3840,128]{1,0:T(8,128)(2,1)} %gene_hbm.3) | copy-start | bytes 2949124
  7.5 71.9 %copy-start.2 = (bf16[512,128]{1,0:T(8,128)(2,1)S(1)}, bf16[512,128]{1,0:T(8,128)(2,1)}, u32[]{:S(2)}) copy-start(bf16[512,128]{1,0:T(8,128)(2,1)} %cell_ref.1) | copy-start | bytes 393220
  7.5 71.9 %copy-start.3 = (s32[1,1,96]{2,1,0:T(1,128)S(1)}, s32[1,1,96]{2,1,0:T(1,128)}, u32[]{:S(2)}) copy-start(s32[1,1,96]{2,1,0:T(1,128)} %param.6) | copy-start | bytes 1156

commit v3 on v2

--- a/solution.py
+++ b/solution.py
@@ -18,6 +18,7 @@
 HBM = pl.BlockSpec(memory_space=pltpu.HBM)
 GROUP = 15
 PIECES = 4
+INNER = 4
 
 
 def dot(a, b, dims=NN):
@@ -62,14 +63,13 @@
 
 
 def residual_pair(vals_ref, pos_ref, resid_ref, cells_ref, genes, first, gene_blocks, at):
-    slots, blk, _ = vals_ref.shape
+    blk = vals_ref.shape[1]
+    whole = dot(cells_ref[...], genes, NT)
     for c in range(cells_ref.shape[0] // blk):
         rows = pl.ds(c * blk, blk)
-        fit = dot(cells_ref[rows, :], genes, NT)
+        fit = whole[c * blk : (c + 1) * blk, :]
         for h in range(2):
-            slot = pos_ref[c * gene_blocks + first + h]
-            live = (slot < slots).astype(F32)
-            value = vals_ref[jnp.minimum(slot, slots - 1)].astype(F32) * live
+            value = vals_ref[pos_ref[c * gene_blocks + first + h]].astype(F32)
             part = value - fit[:, h * blk : (h + 1) * blk]
             to = pl.ds((at + h) * blk, blk)
             resid_ref[rows, to] = jnp.where(value != 0.0, part, 0.0).astype(BF16)
@@ -83,6 +83,7 @@
     share = gene_blocks * blk // owners
     values, others = start_loads(sem, [(vals_hbm, vals_ref), (gene_hbm, gene_ref), (cell_hbm, cell_ref)])
     fill_positions(ids_ref, count_ref, pos_ref)
+    vals_ref[vals_hbm.shape[0]] = jnp.zeros(vals_ref.shape[1:], BF16)
     others[1].wait()
     scaled = cell_ref[...].astype(F32) * scale
     turned_ref[...] = scaled.T.astype(BF16)
@@ -124,7 +125,7 @@
         scratch_shapes=[
             pltpu.SemaphoreType.DMA((PIECES + 2,)),
             pltpu.SMEM((rows // blk * gene_blocks,), jnp.int32),
-            pltpu.VMEM(values.shape, BF16),
+            pltpu.VMEM((slots + 1, blk, blk), BF16),
             pltpu.VMEM(cells.shape, BF16),
             pltpu.VMEM(genes.shape, BF16),
             pltpu.VMEM((rank, rows), BF16),
@@ -137,32 +138,28 @@
 
 
 def add_up_kernel(share, parts_ref, out_ref):
-    parts, height, _ = parts_ref.shape
-    step = share // 4 if share % 32 == 0 else share // 5
-    low = 0
-    while low < share:
-        rows = pl.ds(low, step)
-        total = parts_ref[0, rows, :].astype(F32)
-        for i in range(1, parts):
-            total = total + parts_ref[i, rows, :].astype(F32)
-        total = total.astype(BF16)
-        for i in range(out_ref.shape[0]):
-            out_ref[i, rows, :] = total
-        low += step
-    rows = pl.ds(share, height - share)
-    total = parts_ref[0, rows, :].astype(F32)
-    for i in range(1, parts):
-        total = total + parts_ref[i, rows, :].astype(F32)
+    parts, slots, height, _ = parts_ref.shape
+    pieces = 4 if share % 32 == 0 else 5
+    step = share // pieces
     half = (height - share) // 2
-    gram = two_terms(total[:half, :] + total[half:, :])
-    for i in range(out_ref.shape[0]):
-        out_ref[i, rows, :] = gram
-
-
-def add_up(share, parts):
+    for slot in range(slots):
+        for low in range(0, share + step, step):
+            rows = pl.ds(low, step if low < share else height - share)
+            total = parts_ref[0, slot, rows, :].astype(F32)
+            for i in range(1, parts):
+                total = total + parts_ref[i, slot, rows, :].astype(F32)
+            if low < share:
+                total = total.astype(BF16)
+            else:
+                total = two_terms(total[:half, :] + total[half:, :])
+            for i in range(out_ref.shape[0]):
+                out_ref[i, slot, rows, :] = total
+
+
+def add_up(share, copies, parts):
     return pl.pallas_call(
         functools.partial(add_up_kernel, share),
-        out_shape=jax.ShapeDtypeStruct(parts.shape, BF16),
+        out_shape=jax.ShapeDtypeStruct((copies,) + parts.shape[1:], BF16),
         in_specs=[VMEM],
         out_specs=VMEM,
         compiler_params=PARAMS,
@@ -245,6 +242,7 @@
     senders, height, _ = sums_ref.shape
     values, others = start_loads(sem, [(vals_hbm, vals_ref), (gene_hbm, gene_ref), (cell_hbm, cell_ref)])
     fill_positions(ids_ref, count_ref, pos_ref)
+    vals_ref[vals_hbm.shape[0]] = jnp.zeros(vals_ref.shape[1:], BF16)
     half = (height - share) // 2
     for i in range(senders):
         flat_ref[i * share : (i + 1) * share, :] = sums_ref[i, :share, :]
@@ -311,7 +309,7 @@
             pltpu.SemaphoreType.DMA((PIECES + 2,)),
             pltpu.SemaphoreType.DMA((gene_blocks // (2 * GROUP),)),
             pltpu.SMEM((rows // blk * gene_blocks,), jnp.int32),
-            pltpu.VMEM(values.shape, BF16),
+            pltpu.VMEM((slots + 1, blk, blk), BF16),
             pltpu.VMEM(cells.shape, BF16),
             pltpu.VMEM(genes.shape, BF16),
             pltpu.VMEM(genes.shape, BF16),
@@ -361,8 +359,21 @@
     )(cells, sums)
 
 
-def exchange(parts, axes):
-    return lax.all_to_all(parts, axes, 0, 0, tiled=True)
+def exchange(parts, axis, groups=None):
+    return lax.all_to_all(parts, axis, 0, 0, tiled=True, axis_index_groups=groups)
+
+
+def across_cells(share, terms):
+    owners, height, width = terms.shape
+    outer = owners // INNER
+    inner_groups = [[o * INNER + i for i in range(INNER)] for o in range(outer)]
+    outer_groups = [[o * INNER + i for o in range(outer)] for i in range(INNER)]
+    terms = terms.reshape(INNER, outer, height, width)
+    terms = add_up(share, 1, exchange(terms, "cell", inner_groups))[0]
+    terms = add_up(share, outer, exchange(terms, "cell", outer_groups)[:, None])[:, 0]
+    terms = exchange(terms, "cell", outer_groups)
+    terms = exchange(add_up(share, INNER, terms[None]), "cell", inner_groups)
+    return terms.reshape(owners, height, width)
 
 
 def body(block_values, block_ids, block_count, cell_factor, gene_factor):
@@ -376,9 +387,9 @@
     cell_share = rows // n_gene
 
     terms = first_pass(scale, n_cell, ids, count, values, cell_factor, gene_factor)
-    sums = exchange(add_up(gene_share, exchange(terms, "cell")), "cell")
+    sums = across_cells(gene_share, terms)
     new_genes, cell_terms = second_pass(scale, gene_share, n_gene, ids, count, values, cell_factor, gene_factor, sums)
-    cell_sums = exchange(add_up(cell_share, exchange(cell_terms, "gene")), "gene")
+    cell_sums = exchange(add_up(cell_share, n_gene, exchange(cell_terms, "gene")[:, None])[:, 0], "gene")
     new_cells = make_new_cells(scale, cell_share, cell_factor, cell_sums)
     return new_cells, new_genes
 

time: 148 us -> 139 us (0.939)
  blocking collectives: 106 us -> 99 us
  Pallas kernels: 40.9 us -> 38 us
    all_to_all x4 -> x6, blocking collectives: 106 us -> 99 us  [exchange(): lax.all_to_all(parts, axis, 0, 0, tiled=True, axis_index_groups=groups)]
    pallas_call x1, Pallas kernels: 21.2 us -> 18.5 us  [second_pass(): pl.pallas_call(functools.partial(second_pass_kernel, scale, share), out_s...]
where the time goes in v3:
time: 139 us; the launch traced here: 138 us
  blocking collectives  99 us (71%)
  Pallas kernels  38 us (27%)
    all_to_all x6, blocking collectives, exchange(): lax.all_to_all(parts, axis, 0, 0, tiled=True, axis_index_groups=groups)  99 us
    pallas_call x1, Pallas kernels, second_pass(): pl.pallas_call(functools.partial(second_pass_kernel, scale, share), out_s...  18.5 us
    pallas_call x1, Pallas kernels, make_new_cells(): pl.pallas_call(functools.partial(new_cells_kernel, scale, share), out_sha...  13.2 us
    pallas_call x1, Pallas kernels, first_pass(): pl.pallas_call(functools.partial(first_pass_kernel, scale, gene_blocks),...  5.98 us

profile of v3, /device:TPU:1, one launch (start us, length us, event | category | flops | bytes accessed | tf_op | source)
XLA Modules:
  0.0 138.3 jit_solution(7833494271839969898)
XLA Ops:
  1.3 6.0 %first_pass.1 = bf16[32,128,128]{2,1,0:T(8,128)(2,1)} custom-call(s32[96]{0:T(128)} %bitcast.22, s32[1]{0:T(128)} %bitcast.11.count_ref, bf16[96,128,128]{2,1,0:T(8,128)(2,1)} %bitcast.13, bf16[512,128]{1,0:T(8,128)(2,1)} %cell_ref.1, bf16[3840,128]{1,0:T(8,128)(2,1)} %gene_hbm.3), custom_call_target="tpu_custom_call" | custom-call | tf_op jit(solution)/shard_map/first_pass/pallas_call | solution.py:120
  7.3 14.6 %all_to_all.30.parts_ref = bf16[4,8,128,128]{3,2,1,0:T(8,128)(2,1)S(1)} all-to-all(bf16[4,8,128,128]{3,2,1,0:T(8,128)(2,1)} %bitcast.24), channel_id=1, replica_groups={{0,16,32,48},{64,80,96,112},{128,144,160,176},{192,208,224,240},{256,27..., dimensions={0} | all-to-all | bytes 2097152 | tf_op jit(solution)/shard_map/all_to_all | solution.py:363
  21.9 0.0 copy-start
  21.9 0.0 copy-start.1
  21.9 0.0 copy-start.2
  21.9 0.0 copy-start.3
  21.9 0.1 add_up.4
  22.0 23.9 %all_to_all.31 = bf16[8,128,128]{2,1,0:T(8,128)(2,1)S(1)} all-to-all(bf16[8,128,128]{2,1,0:T(8,128)(2,1)S(1)} %bitcast.16), channel_id=1, replica_groups={{0,64,128,192,256,320,384,448},{16,80,144,208,272,336,400,464},{32,96,1..., dimensions={0} | all-to-all | bytes 524288 | tf_op jit(solution)/shard_map/all_to_all | solution.py:363
  45.9 11.8 %all_to_all.32 = bf16[8,128,128]{2,1,0:T(8,128)(2,1)S(1)} all-to-all(bf16[8,128,128]{2,1,0:T(8,128)(2,1)S(1)} %bitcast.19), channel_id=1, replica_groups={{0,64,128,192,256,320,384,448},{16,80,144,208,272,336,400,464},{32,96,1..., dimensions={0} | all-to-all | bytes 524288 | tf_op jit(solution)/shard_map/all_to_all | solution.py:363
  57.8 0.1 add_up.6
  57.9 13.0 %all_to_all.33 = bf16[4,8,128,128]{3,2,1,0:T(8,128)(2,1)S(1)} all-to-all(bf16[4,8,128,128]{3,2,1,0:T(8,128)(2,1)S(1)} %add_up.6), channel_id=1, replica_groups={{0,16,32,48},{64,80,96,112},{128,144,160,176},{192,208,224,240},{256,27..., dimensions={0} | all-to-all | bytes 2097152 | tf_op jit(solution)/shard_map/all_to_all | solution.py:363
  70.9 0.0 copy-done
  70.9 0.0 copy-done.1
  70.9 0.0 copy-done.2
  70.9 0.0 copy-done.3
  70.9 18.5 %second_pass.1 = (bf16[3840,128]{1,0:T(8,128)(2,1)}, bf16[16,48,128]{2,1,0:T(8,128)(2,1)S(1)}) custom-call(s32[96]{0:T(128)S(1)} %bitcast.23, s32[1]{0:T(128)} %bitcast.12.count_ref, bf16[96,128,128]{2,1,0:T(8,128)(2,1)S(1)} %bitcast.14, bf16[512,128]{1,0:T(8,128)(2,1)S(1)} %copy-done.2, bf16[3840,128]{1,0:T(8,128)(2,1)S(1)} %copy-done.1, ...), custom_call_target="tpu_custom_call" | custom-call | tf_op jit(solution)/shard_map/second_pass/pallas_call | solution.py:303
  89.4 22.7 %all_to_all.34 = bf16[16,48,128]{2,1,0:T(8,128)(2,1)S(1)} all-to-all(bf16[16,48,128]{2,1,0:T(8,128)(2,1)S(1)} %get-tuple-element.4), channel_id=1, replica_groups=mesh['cell'=32,'gene'=16] {'gene'}, dimensions={0} | all-to-all | bytes 393216 | tf_op jit(solution)/shard_map/all_to_all | solution.py:363
  112.2 13.0 %all_to_all.35.sums_ref = bf16[16,48,128]{2,1,0:T(8,128)(2,1)S(1)} all-to-all(bf16[16,48,128]{2,1,0:T(8,128)(2,1)S(1)} %bitcast.21), channel_id=1, replica_groups=mesh['cell'=32,'gene'=16] {'gene'}, dimensions={0} | all-to-all | bytes 393216 | tf_op jit(solution)/shard_map/all_to_all | solution.py:363
  125.1 13.2 %new_cells.1 = bf16[512,128]{1,0:T(8,128)(2,1)} custom-call(bf16[512,128]{1,0:T(8,128)(2,1)S(1)} %copy-done.2, bf16[16,48,128]{2,1,0:T(8,128)(2,1)S(1)} %all_to_all.35.sums_ref), custom_call_target="tpu_custom_call" | custom-call | tf_op jit(solution)/shard_map/new_cells/pallas_call | solution.py:347
  (2 shorter events, 0.1 us)
Async XLA Ops:
  21.9 49.0 %copy-start = (bf16[1,1,96,128,128]{4,3,2,1,0:T(8,128)(2,1)S(1)}, bf16[1,1,96,128,128]{4,3,2,1,0:T(8,128)(2,1)}, u32[]{:S(2)}) copy-start(bf16[1,1,96,128,128]{4,3,2,1,0:T(8,128)(2,1)} %param.5) | copy-start | bytes 9437188
  21.9 49.0 %copy-start.1 = (bf16[3840,128]{1,0:T(8,128)(2,1)S(1)}, bf16[3840,128]{1,0:T(8,128)(2,1)}, u32[]{:S(2)}) copy-start(bf16[3840,128]{1,0:T(8,128)(2,1)} %gene_hbm.3) | copy-start | bytes 2949124
  21.9 49.0 %copy-start.2 = (bf16[512,128]{1,0:T(8,128)(2,1)S(1)}, bf16[512,128]{1,0:T(8,128)(2,1)}, u32[]{:S(2)}) copy-start(bf16[512,128]{1,0:T(8,128)(2,1)} %cell_ref.1) | copy-start | bytes 393220
  21.9 49.0 %copy-start.3 = (s32[1,1,96]{2,1,0:T(1,128)S(1)}, s32[1,1,96]{2,1,0:T(1,128)}, u32[]{:S(2)}) copy-start(s32[1,1,96]{2,1,0:T(1,128)} %param.6) | copy-start | bytes 1156

commit v4 on v3

v4 whole, which is shorter than its diff:
```python
import functools

import jax
import jax.numpy as jnp
from jax import lax
from jax.experimental import pallas as pl
from jax.experimental.pallas import tpu as pltpu
from jax.sharding import PartitionSpec as P

LAMBDA = 0.5
F32 = jnp.float32
BF16 = jnp.bfloat16
NN = (((1,), (0,)), ((), ()))
NT = (((1,), (1,)), ((), ()))
PARAMS = pltpu.CompilerParams(vmem_limit_bytes=48 * 1024 * 1024)
SMEM = pl.BlockSpec(memory_space=pltpu.SMEM)
VMEM = pl.BlockSpec(memory_space=pltpu.VMEM)
HBM = pl.BlockSpec(memory_space=pltpu.HBM)
FIRST_STAGES = (5, 10, 15)
SECOND_STAGES = (15,)
AHEAD = 8
PIECES = 4
INNER = 4


def dot(a, b, dims=NN):
    return lax.dot_general(a, b, dims, preferred_element_type=F32)


def exact_dot(a, b):
    return lax.dot_general(a, b, NN, precision=lax.Precision.HIGHEST, preferred_element_type=F32)


def split(value):
    high = value.astype(BF16)
    return high, (value - high.astype(F32)).astype(BF16)


def two_terms(value):
    high = value.astype(BF16).astype(F32)
    return jnp.concatenate([high, value - high], axis=0).astype(BF16)


def start_loads(sem, small, large):
    copies = [pltpu.make_async_copy(source, target, sem.at[i]) for i, (source, target) in enumerate(small)]
    source, target = large
    step = source.shape[0] // PIECES
    for i in range(PIECES):
        part = pl.ds(i * step, step)
        copies.append(pltpu.make_async_copy(source.at[part], target.at[part], sem.at[len(small) + i]))
    for copy in copies:
        copy.start()
    return copies[: len(small)], copies[len(small) :]


def fill_positions(ids_ref, count_ref, pos_ref):
    slots = ids_ref.shape[0]
    for i in range(pos_ref.shape[0]):
        pos_ref[i] = slots
    count = count_ref[0]
    for k in range(slots):
        pos_ref[ids_ref[k]] = jnp.where(k < count, k, slots)


def residual_pair(vals_ref, pos_ref, resid_ref, fit, first, gene_blocks, at):
    blk = vals_ref.shape[1]
    for c in range(fit.shape[0] // blk):
        for h in range(2):
            value = vals_ref[pos_ref[c * gene_blocks + first + h]].astype(F32)
            part = value - fit[c * blk : (c + 1) * blk, h * blk : (h + 1) * blk]
            to = pl.ds((at + h) * blk, blk)
            resid_ref[pl.ds(c * blk, blk), to] = jnp.where(value != 0.0, part, 0.0).astype(BF16)


def first_pass_kernel(
    scale,
    gene_blocks,
    ids_hbm,
    count_ref,
    vals_hbm,
    cell_hbm,
    gene_hbm,
    out_hbm,
    sem,
    out_sem,
    ids_ref,
    pos_ref,
    vals_ref,
    cell_ref,
    gene_ref,
    turned_ref,
    fit_ref,
    resid_ref,
    out_ref,
):
    blk = vals_ref.shape[1]
    rank = cell_ref.shape[1]
    small, values = start_loads(
        sem, [(ids_hbm, ids_ref), (cell_hbm, cell_ref), (gene_hbm, gene_ref)], (vals_hbm, vals_ref.at[: vals_hbm.shape[0]])
    )
    vals_ref[vals_hbm.shape[0]] = jnp.zeros(vals_ref.shape[1:], BF16)
    small[1].wait()
    scaled = cell_ref[...].astype(F32) * scale
    turned_ref[...] = scaled.T.astype(BF16)
    cell_ref[...] = scaled.astype(BF16)
    gram = dot(turned_ref[...], cell_ref[...])
    out_ref[gene_blocks] = two_terms(gram[: rank // 2, :])
    out_ref[gene_blocks + 1] = two_terms(gram[rank // 2 :, :])
    small[2].wait()

    def fit_of(pair):
        return dot(cell_ref[...], gene_ref[2 * pair * blk : 2 * (pair + 1) * blk, :], NT)

    ahead = fit_ref.shape[0]
    for pair in range(ahead):
        fit_ref[pair] = fit_of(pair)
    small[0].wait()
    fill_positions(ids_ref, count_ref, pos_ref)
    for copy in values:
        copy.wait()

    stores = []
    low = 0
    for high in FIRST_STAGES:
        for pair in range(low, high):
            fit = fit_ref[pair] if pair < ahead else fit_of(pair)
            residual_pair(vals_ref, pos_ref, resid_ref, fit, 2 * pair, gene_blocks, 2 * pair)
        terms = dot(turned_ref[...], resid_ref[:, 2 * low * blk : 2 * high * blk]).astype(BF16)
        for u in range(2 * (high - low)):
            out_ref[2 * low + u] = terms[:, u * blk : (u + 1) * blk]
        to = pl.ds(2 * low, 2 * (high - low) + (2 if high == FIRST_STAGES[-1] else 0))
        stores.append(pltpu.make_async_copy(out_ref.at[to], out_hbm.at[to], out_sem.at[len(stores)]))
        stores[-1].start()
        low = high
    for store in stores:
        store.wait()


def first_pass(scale, ids, count, values, cells, genes):
    slots, blk, _ = values.shape
    rows, rank = cells.shape
    gene_blocks = genes.shape[0] // blk
    return pl.pallas_call(
        functools.partial(first_pass_kernel, scale, gene_blocks),
        out_shape=jax.ShapeDtypeStruct((gene_blocks + 2, rank, blk), BF16),
        in_specs=[HBM, SMEM, HBM, HBM, HBM],
        out_specs=HBM,
        scratch_shapes=[
            pltpu.SemaphoreType.DMA((PIECES + 3,)),
            pltpu.SemaphoreType.DMA((len(FIRST_STAGES),)),
            pltpu.SMEM((slots,), jnp.int32),
            pltpu.SMEM((rows // blk * gene_blocks,), jnp.int32),
            pltpu.VMEM((slots + 1, blk, blk), BF16),
            pltpu.VMEM(cells.shape, BF16),
            pltpu.VMEM(genes.shape, BF16),
            pltpu.VMEM((rank, rows), BF16),
            pltpu.VMEM((AHEAD, rows, 2 * blk), F32),
            pltpu.VMEM((rows, genes.shape[0]), BF16),
            pltpu.VMEM((gene_blocks + 2, rank, blk), BF16),
        ],
        compiler_params=pltpu.CompilerParams(vmem_limit_bytes=63 * 1024 * 1024),
        name="first_pass",
    )(ids, count, values, cells, genes)


def total_of(parts_ref, slot, rows):
    total = parts_ref[0, slot, rows, :].astype(F32)
    for i in range(1, parts_ref.shape[0]):
        total = total + parts_ref[i, slot, rows, :].astype(F32)
    return total


def add_blocks_kernel(stage, gram_from, parts_ref, out_ref):
    parts, slots, height, _ = parts_ref.shape
    place = lax.axis_index("cell")
    outer = lax.axis_size("cell") // INNER
    first = (place % INNER) * outer + (place // INNER if stage else 0)
    step = height // 4
    for slot in range(slots):
        may_be_gram = stage or slot >= gram_from % outer
        if may_be_gram:
            whole = total_of(parts_ref, slot, pl.ds(0, height))
            is_gram = first + slot >= gram_from
            gram = two_terms(whole[: height // 2, :] + whole[height // 2 :, :]).astype(F32)
            whole = jnp.where(is_gram, gram, whole).astype(BF16)
            for i in range(out_ref.shape[0]):
                out_ref[i, slot] = whole
        else:
            for low in range(0, height, step):
                rows = pl.ds(low, step)
                out_ref[0, slot, rows, :] = total_of(parts_ref, slot, rows).astype(BF16)


def add_blocks(stage, copies, gram_from, parts):
    return pl.pallas_call(
        functools.partial(add_blocks_kernel, stage, gram_from),
        out_shape=jax.ShapeDtypeStruct((copies,) + parts.shape[1:], BF16),
        in_specs=[VMEM],
        out_specs=VMEM,
        compiler_params=PARAMS,
        name="add_blocks",
    )(parts)


def repeat_kernel(part_ref, out_ref):
    for slot in range(part_ref.shape[0]):
        block = part_ref[slot]
        for i in range(out_ref.shape[0]):
            out_ref[i, slot] = block


def repeat(copies, part):
    return pl.pallas_call(
        repeat_kernel,
        out_shape=jax.ShapeDtypeStruct((copies,) + part.shape, BF16),
        in_specs=[VMEM],
        out_specs=VMEM,
        compiler_params=PARAMS,
        name="repeat",
    )(part)


def add_cells_kernel(share, parts_ref, out_ref):
    senders, height, _ = parts_ref.shape

    def total(rows):
        value = parts_ref[0, rows, :].astype(F32)
        for i in range(1, senders):
            value = value + parts_ref[i, rows, :].astype(F32)
        return value

    cells = total(pl.ds(0, share)).astype(BF16)
    gram = two_terms(total(pl.ds(share, height - share)))
    for i in range(out_ref.shape[0]):
        out_ref[i, :share, :] = cells
        out_ref[i, share:, :] = gram


def add_cells(share, parts):
    senders, height, rank = parts.shape
    return pl.pallas_call(
        functools.partial(add_cells_kernel, share),
        out_shape=jax.ShapeDtypeStruct((senders, 2 * height - share, rank), BF16),
        in_specs=[VMEM],
        out_specs=VMEM,
        compiler_params=PARAMS,
        name="add_cells",
    )(parts)


def eliminate(work, row, column):
    for k in range(work.shape[0]):
        at_row = row[:, 0:1] == k
        at_column = column[0:1, :] == k
        line = work[k : k + 1, :]
        pivot = 1.0 / work[k : k + 1, k : k + 1]
        side = work[:, k : k + 1] - jnp.where(at_row, 1.0, 0.0)
        line = jnp.where(at_column, 1.0, line) * pivot
        kept = jnp.where(at_column, jnp.where(at_row, 1.0, 0.0), work)
        work = kept - side * line
    return work


def solve_into(solve_ref, inverse_ref, gram):
    rank = gram.shape[0]
    row = lax.broadcasted_iota(jnp.int32, (rank, rank), 0)
    column = lax.broadcasted_iota(jnp.int32, (rank, rank), 1)
    diagonal = row == column
    eye = jnp.where(diagonal, 1.0, 0.0)
    matrix = gram + LAMBDA * eye
    along = jnp.where(diagonal, matrix, 0.0)
    down = 1.0 / jnp.sum(along, axis=1, keepdims=True)
    across = 1.0 / jnp.sum(along, axis=0, keepdims=True)
    off = (eye - matrix * across).astype(BF16)
    guess = (eye + (eye - matrix * across)) * down
    guess = guess + dot(guess.astype(BF16), dot(off, off).astype(BF16))
    rest = eye - exact_dot(matrix, guess)
    inverse_ref[...] = guess + exact_dot(guess, rest)
    size = jnp.sum(rest * rest)

    @pl.when(jnp.logical_not(size < 4e-6))
    def _():
        inverse_ref[...] = eliminate(matrix, row, column)

    inverse = inverse_ref[...]
    high, low = split(exact_dot(inverse, gram))
    solve_ref[:, 0:rank] = high
    solve_ref[:, rank : 2 * rank] = low
    high, low = split(inverse)
    solve_ref[:, 2 * rank : 3 * rank] = high
    solve_ref[:, 3 * rank : 4 * rank] = low


def second_pass_kernel(
    scale,
    ids_hbm,
    count_ref,
    vals_hbm,
    cell_hbm,
    gene_hbm,
    sums_ref,
    new_hbm,
    out_ref,
    sem,
    out_sem,
    ids_ref,
    pos_ref,
    vals_ref,
    cell_ref,
    gene_ref,
    solve_ref,
    new_ref,
    turned_ref,
    resid_ref,
    total_ref,
):
    blk = vals_ref.shape[1]
    rank = cell_ref.shape[1]
    gene_blocks = gene_ref.shape[0] // blk
    small, values = start_loads(
        sem, [(ids_hbm, ids_ref), (cell_hbm, cell_ref), (gene_hbm, gene_ref)], (vals_hbm, vals_ref.at[: vals_hbm.shape[0]])
    )
    vals_ref[vals_hbm.shape[0]] = jnp.zeros(vals_ref.shape[1:], BF16)
    small[0].wait()
    fill_positions(ids_ref, count_ref, pos_ref)
    halves = [sums_ref[gene_blocks + i].astype(F32) for i in range(2)]
    gram = jnp.concatenate([half[: rank // 2, :] + half[rank // 2 :, :] for half in halves], axis=0)
    solve_into(solve_ref, total_ref.at[:rank, :], gram)
    for copy in small[1:] + values:
        copy.wait()
    cell_ref[...] = (cell_ref[...].astype(F32) * scale).astype(BF16)
    total_ref[...] = jnp.zeros_like(total_ref)
    stores = []
    low = 0
    for high in SECOND_STAGES:
        for pair in range(low, high):
            rows = pl.ds(2 * pair * blk, 2 * blk)
            sums = jnp.concatenate([sums_ref[2 * pair], sums_ref[2 * pair + 1]], axis=1)
            old = gene_ref[rows, :]
            turned = (
                dot(solve_ref[:, 0:rank], old, NT)
                + dot(solve_ref[:, rank : 2 * rank], old, NT)
                + dot(solve_ref[:, 2 * rank : 4 * rank], jnp.concatenate([sums, sums], axis=0))
            )
            genes = turned.T.astype(BF16)
            turned_ref[:, rows] = turned.astype(BF16)
            new_ref[rows, :] = genes
            residual_pair(vals_ref, pos_ref, resid_ref, dot(cell_ref[...], genes, NT), 2 * pair, gene_blocks, 2 * pair)
        rows = pl.ds(2 * low * blk, 2 * (high - low) * blk)
        total_ref[...] += dot(resid_ref[:, rows], new_ref[rows, :])
        stores.append(pltpu.make_async_copy(new_ref.at[rows], new_hbm.at[rows], out_sem.at[len(stores)]))
        stores[-1].start()
        low = high
    gram = dot(turned_ref[...], new_ref[...])
    owners, out_height, _ = out_ref.shape
    count = total_ref.shape[0] // owners
    lines = out_height - count
    for i in range(owners):
        out_ref[i, :count, :] = total_ref[i * count : (i + 1) * count, :].astype(BF16)
        out_ref[i, count:, :] = gram[i * lines : (i + 1) * lines, :].astype(BF16)
    for store in stores:
        store.wait()


def second_pass(scale, owners, ids, count, values, cells, genes, sums):
    slots, blk, _ = values.shape
    rows, rank = cells.shape
    gene_blocks = genes.shape[0] // blk
    height = (rows + rank) // owners
    return pl.pallas_call(
        functools.partial(second_pass_kernel, scale),
        out_shape=(jax.ShapeDtypeStruct(genes.shape, BF16), jax.ShapeDtypeStruct((owners, height, rank), BF16)),
        in_specs=[HBM, SMEM, HBM, HBM, HBM, VMEM],
        out_specs=(HBM, VMEM),
        scratch_shapes=[
            pltpu.SemaphoreType.DMA((PIECES + 3,)),
            pltpu.SemaphoreType.DMA((len(SECOND_STAGES),)),
            pltpu.SMEM((slots,), jnp.int32),
            pltpu.SMEM((rows // blk * gene_blocks,), jnp.int32),
            pltpu.VMEM((slots + 1, blk, blk), BF16),
            pltpu.VMEM(cells.shape, BF16),
            pltpu.VMEM(genes.shape, BF16),
            pltpu.VMEM((rank, 4 * rank), BF16),
            pltpu.VMEM(genes.shape, BF16),
            pltpu.VMEM((rank, genes.shape[0]), BF16),
            pltpu.VMEM((rows, genes.shape[0]), BF16),
            pltpu.VMEM((rows, rank), F32),
        ],
        compiler_params=PARAMS,
        name="second_pass",
    )(ids, count, values, cells, genes, sums)


def new_cells_kernel(scale, share, cell_ref, sums_ref, out_ref, solve_ref, gram_ref, inverse_ref):
    rank = cell_ref.shape[1]
    senders, height, _ = sums_ref.shape
    half = (height - share) // 2
    for i in range(senders):
        gram = sums_ref[i, share:, :].astype(F32)
        gram_ref[i * half : (i + 1) * half, :] = gram[:half, :] + gram[half:, :]
    solve_into(solve_ref, inverse_ref, gram_ref[...])
    sums = (sums_ref[:, :share, :].reshape(senders * share, rank).astype(F32) * (1.0 / scale)).astype(BF16)
    out_ref[...] = (
        dot(cell_ref[...], solve_ref[:, 0:rank], NT)
        + dot(cell_ref[...], solve_ref[:, rank : 2 * rank], NT)
        + dot(sums, solve_ref[:, 2 * rank : 3 * rank], NT)
        + dot(sums, solve_ref[:, 3 * rank : 4 * rank], NT)
    ).astype(BF16)


def make_new_cells(scale, share, cells, sums):
    rank = cells.shape[1]
    return pl.pallas_call(
        functools.partial(new_cells_kernel, scale, share),
        out_shape=jax.ShapeDtypeStruct(cells.shape, BF16),
        in_specs=[VMEM] * 2,
        out_specs=VMEM,
        scratch_shapes=[
            pltpu.VMEM((rank, 4 * rank), BF16),
            pltpu.VMEM((rank, rank), F32),
            pltpu.VMEM((rank, rank), F32),
        ],
        compiler_params=PARAMS,
        name="new_cells",
    )(cells, sums)


def exchange(parts, axis, groups=None):
    return lax.all_to_all(parts, axis, 0, 0, tiled=True, axis_index_groups=groups)


def across_cells(blocks):
    owners = blocks.shape[0]
    outer = owners // INNER
    inner_groups = [[o * INNER + i for i in range(INNER)] for o in range(outer)]
    outer_groups = [[o * INNER + i for o in range(outer)] for i in range(INNER)]
    parts = exchange(blocks, "cell", inner_groups).reshape((INNER, outer) + blocks.shape[1:])
    parts = exchange(add_blocks(0, 1, owners - 2, parts)[0], "cell", outer_groups)
    parts = exchange(add_blocks(1, outer, owners - 2, parts[:, None])[:, 0], "cell", outer_groups)
    return exchange(repeat(INNER, parts).reshape(blocks.shape), "cell", inner_groups)


def body(block_values, block_ids, block_count, cell_factor, gene_factor):
    values = block_values[0, 0]
    ids = block_ids[0, 0]
    count = block_count[0]
    rows = cell_factor.shape[0]
    n_cell, n_gene = lax.axis_size("cell"), lax.axis_size("gene")
    scale = (rows * n_cell) ** (-0.5)
    cell_share = rows // n_gene

    sums = across_cells(first_pass(scale, ids, count, values, cell_factor, gene_factor))
    new_genes, cell_terms = second_pass(scale, n_gene, ids, count, values, cell_factor, gene_factor, sums)
    cell_sums = exchange(add_cells(cell_share, exchange(cell_terms, "gene")), "gene")
    new_cells = make_new_cells(scale, cell_share, cell_factor, cell_sums)
    return new_cells, new_genes


def solution(mesh):
    return jax.shard_map(
        body,
        mesh=mesh,
        in_specs=(
            P("cell", "gene", None, None, None),
            P("cell", "gene", None),
            P("cell", "gene"),
            P("cell", None),
            P("gene", None),
        ),
        out_specs=(P("cell", None), P("gene", None)),
        check_vma=False,
    )
```

time: 139 us -> 136 us (0.978)
  Pallas kernels: 38 us -> 35.9 us
where the time goes in v4:
time: 136 us
  blocking collectives  98.3 us (72%)
  Pallas kernels  35.9 us (26%)
    all_to_all x6, blocking collectives, exchange(): lax.all_to_all(parts, axis, 0, 0, tiled=True, axis_index_groups=groups)  98.3 us
    pallas_call x1, Pallas kernels, second_pass(): pl.pallas_call(functools.partial(second_pass_kernel, scale), out_shape=(j...  17.6 us
    pallas_call x1, Pallas kernels, make_new_cells(): pl.pallas_call(functools.partial(new_cells_kernel, scale, share), out_sha...  12.8 us
    pallas_call x1, Pallas kernels, first_pass(): pl.pallas_call(functools.partial(first_pass_kernel, scale, gene_blocks),...  5.09 us

profile of v4, /device:TPU:1, one launch (start us, length us, event | category | flops | bytes accessed | tf_op | source)
XLA Modules:
  0.0 135.5 jit_solution(9507212301092536989)
XLA Ops:
  1.3 5.1 %first_pass.1 = bf16[32,128,128]{2,1,0:T(8,128)(2,1)} custom-call(s32[96]{0:T(128)} %bitcast.17, s32[1]{0:T(128)} %bitcast.8.count_ref, bf16[96,128,128]{2,1,0:T(8,128)(2,1)} %bitcast.10, bf16[512,128]{1,0:T(8,128)(2,1)} %cell_ref.1, bf16[3840,128]{1,0:T(8,128)(2,1)} %gene_hbm.3), custom_call_target="tpu_custom_call" | custom-call | tf_op jit(solution)/shard_map/first_pass/pallas_call | solution.py:143
  6.4 14.6 %all_to_all.30 = bf16[32,128,128]{2,1,0:T(8,128)(2,1)S(1)} all-to-all(bf16[32,128,128]{2,1,0:T(8,128)(2,1)} %first_pass.1), channel_id=1, replica_groups={{0,16,32,48},{64,80,96,112},{128,144,160,176},{192,208,224,240},{256,27..., dimensions={0} | all-to-all | bytes 2097152 | tf_op jit(solution)/shard_map/all_to_all | solution.py:429
  21.0 0.0 copy-start
  21.0 0.0 copy-start.1
  21.0 0.0 copy-start.2
  21.0 0.0 copy-start.3
  21.0 0.1 add_blocks.2
  21.1 23.9 %all_to_all.31 = bf16[8,128,128]{2,1,0:T(8,128)(2,1)S(1)} all-to-all(bf16[8,128,128]{2,1,0:T(8,128)(2,1)S(1)} %bitcast.14), channel_id=1, replica_groups={{0,64,128,192,256,320,384,448},{16,80,144,208,272,336,400,464},{32,96,1..., dimensions={0} | all-to-all | bytes 524288 | tf_op jit(solution)/shard_map/all_to_all | solution.py:429
  45.0 0.1 add_blocks.3
  45.0 11.8 %all_to_all.32.part_ref = bf16[8,128,128]{2,1,0:T(8,128)(2,1)S(1)} all-to-all(bf16[8,128,128]{2,1,0:T(8,128)(2,1)S(1)} %bitcast.16), channel_id=1, replica_groups={{0,64,128,192,256,320,384,448},{16,80,144,208,272,336,400,464},{32,96,1..., dimensions={0} | all-to-all | bytes 524288 | tf_op jit(solution)/shard_map/all_to_all | solution.py:429
  56.9 0.1 repeat.1
  57.0 13.0 %all_to_all.33.sums_ref = bf16[32,128,128]{2,1,0:T(8,128)(2,1)S(1)} all-to-all(bf16[32,128,128]{2,1,0:T(8,128)(2,1)S(1)} %bitcast.13), channel_id=1, replica_groups={{0,16,32,48},{64,80,96,112},{128,144,160,176},{192,208,224,240},{256,27..., dimensions={0} | all-to-all | bytes 2097152 | tf_op jit(solution)/shard_map/all_to_all | solution.py:429
  70.0 0.0 copy-done
  70.0 0.0 copy-done.1
  70.0 0.0 copy-done.2
  70.0 0.0 copy-done.3
  70.0 17.6 %second_pass.1 = (bf16[3840,128]{1,0:T(8,128)(2,1)}, bf16[16,40,128]{2,1,0:T(8,128)(2,1)S(1)}) custom-call(s32[96]{0:T(128)S(1)} %bitcast.18, s32[1]{0:T(128)} %bitcast.9.count_ref, bf16[96,128,128]{2,1,0:T(8,128)(2,1)S(1)} %bitcast.11, bf16[512,128]{1,0:T(8,128)(2,1)S(1)} %copy-done.2, bf16[3840,128]{1,0:T(8,128)(2,1)S(1)} %copy-done.1, ...), custom_call_target="tpu_custom_call" | custom-call | tf_op jit(solution)/shard_map/second_pass/pallas_call | solution.py:370
  87.6 22.1 %all_to_all.34.parts_ref = bf16[16,40,128]{2,1,0:T(8,128)(2,1)S(1)} all-to-all(bf16[16,40,128]{2,1,0:T(8,128)(2,1)S(1)} %get-tuple-element.4), channel_id=1, replica_groups=mesh['cell'=32,'gene'=16] {'gene'}, dimensions={0} | all-to-all | bytes 327680 | tf_op jit(solution)/shard_map/all_to_all | solution.py:429
  109.7 13.0 %all_to_all.35.sums_ref = bf16[16,48,128]{2,1,0:T(8,128)(2,1)S(1)} all-to-all(bf16[16,48,128]{2,1,0:T(8,128)(2,1)S(1)} %add_cells.1), channel_id=1, replica_groups=mesh['cell'=32,'gene'=16] {'gene'}, dimensions={0} | all-to-all | bytes 393216 | tf_op jit(solution)/shard_map/all_to_all | solution.py:429
  122.7 12.8 %new_cells.1 = bf16[512,128]{1,0:T(8,128)(2,1)} custom-call(bf16[512,128]{1,0:T(8,128)(2,1)S(1)} %copy-done.2, bf16[16,48,128]{2,1,0:T(8,128)(2,1)S(1)} %all_to_all.35.sums_ref), custom_call_target="tpu_custom_call" | custom-call | tf_op jit(solution)/shard_map/new_cells/pallas_call | solution.py:413
  (1 shorter events, 0.0 us)
Async XLA Ops:
  21.0 49.0 %copy-start = (bf16[1,1,96,128,128]{4,3,2,1,0:T(8,128)(2,1)S(1)}, bf16[1,1,96,128,128]{4,3,2,1,0:T(8,128)(2,1)}, u32[]{:S(2)}) copy-start(bf16[1,1,96,128,128]{4,3,2,1,0:T(8,128)(2,1)} %param.5) | copy-start | bytes 9437188
  21.0 49.0 %copy-start.1 = (bf16[3840,128]{1,0:T(8,128)(2,1)S(1)}, bf16[3840,128]{1,0:T(8,128)(2,1)}, u32[]{:S(2)}) copy-start(bf16[3840,128]{1,0:T(8,128)(2,1)} %gene_hbm.3) | copy-start | bytes 2949124
  21.0 49.0 %copy-start.2 = (bf16[512,128]{1,0:T(8,128)(2,1)S(1)}, bf16[512,128]{1,0:T(8,128)(2,1)}, u32[]{:S(2)}) copy-start(bf16[512,128]{1,0:T(8,128)(2,1)} %cell_ref.1) | copy-start | bytes 393220
  21.0 49.0 %copy-start.3 = (s32[1,1,96]{2,1,0:T(1,128)S(1)}, s32[1,1,96]{2,1,0:T(1,128)}, u32[]{:S(2)}) copy-start(s32[1,1,96]{2,1,0:T(1,128)} %param.6) | copy-start | bytes 1156

commit v5 on v4

--- a/solution.py
+++ b/solution.py
@@ -17,9 +17,8 @@
 VMEM = pl.BlockSpec(memory_space=pltpu.VMEM)
 HBM = pl.BlockSpec(memory_space=pltpu.HBM)
 FIRST_STAGES = (5, 10, 15)
-SECOND_STAGES = (15,)
 AHEAD = 8
-PIECES = 4
+PIECES = 1
 INNER = 4
 
 
@@ -220,27 +219,19 @@
     )(part)
 
 
-def add_cells_kernel(share, parts_ref, out_ref):
-    senders, height, _ = parts_ref.shape
-
-    def total(rows):
-        value = parts_ref[0, rows, :].astype(F32)
-        for i in range(1, senders):
-            value = value + parts_ref[i, rows, :].astype(F32)
-        return value
-
-    cells = total(pl.ds(0, share)).astype(BF16)
-    gram = two_terms(total(pl.ds(share, height - share)))
+def add_cells_kernel(parts_ref, out_ref):
+    value = parts_ref[0].astype(F32)
+    for i in range(1, parts_ref.shape[0]):
+        value = value + parts_ref[i].astype(F32)
+    total = value.astype(BF16)
     for i in range(out_ref.shape[0]):
-        out_ref[i, :share, :] = cells
-        out_ref[i, share:, :] = gram
-
-
-def add_cells(share, parts):
-    senders, height, rank = parts.shape
-    return pl.pallas_call(
-        functools.partial(add_cells_kernel, share),
-        out_shape=jax.ShapeDtypeStruct((senders, 2 * height - share, rank), BF16),
+        out_ref[i] = total
+
+
+def add_cells(parts):
+    return pl.pallas_call(
+        add_cells_kernel,
+        out_shape=jax.ShapeDtypeStruct(parts.shape, BF16),
         in_specs=[VMEM],
         out_specs=VMEM,
         compiler_params=PARAMS,
@@ -326,40 +317,37 @@
     halves = [sums_ref[gene_blocks + i].astype(F32) for i in range(2)]
     gram = jnp.concatenate([half[: rank // 2, :] + half[rank // 2 :, :] for half in halves], axis=0)
     solve_into(solve_ref, total_ref.at[:rank, :], gram)
-    for copy in small[1:] + values:
+    for copy in small[1:]:
         copy.wait()
     cell_ref[...] = (cell_ref[...].astype(F32) * scale).astype(BF16)
-    total_ref[...] = jnp.zeros_like(total_ref)
-    stores = []
-    low = 0
-    for high in SECOND_STAGES:
-        for pair in range(low, high):
-            rows = pl.ds(2 * pair * blk, 2 * blk)
-            sums = jnp.concatenate([sums_ref[2 * pair], sums_ref[2 * pair + 1]], axis=1)
-            old = gene_ref[rows, :]
-            turned = (
-                dot(solve_ref[:, 0:rank], old, NT)
-                + dot(solve_ref[:, rank : 2 * rank], old, NT)
-                + dot(solve_ref[:, 2 * rank : 4 * rank], jnp.concatenate([sums, sums], axis=0))
-            )
-            genes = turned.T.astype(BF16)
-            turned_ref[:, rows] = turned.astype(BF16)
-            new_ref[rows, :] = genes
-            residual_pair(vals_ref, pos_ref, resid_ref, dot(cell_ref[...], genes, NT), 2 * pair, gene_blocks, 2 * pair)
-        rows = pl.ds(2 * low * blk, 2 * (high - low) * blk)
-        total_ref[...] += dot(resid_ref[:, rows], new_ref[rows, :])
-        stores.append(pltpu.make_async_copy(new_ref.at[rows], new_hbm.at[rows], out_sem.at[len(stores)]))
-        stores[-1].start()
-        low = high
+    pairs = gene_blocks // 2
+    for pair in range(pairs):
+        rows = pl.ds(2 * pair * blk, 2 * blk)
+        sums = jnp.concatenate([sums_ref[2 * pair], sums_ref[2 * pair + 1]], axis=1)
+        old = gene_ref[rows, :]
+        turned = (
+            dot(solve_ref[:, 0:rank], old, NT)
+            + dot(solve_ref[:, rank : 2 * rank], old, NT)
+            + dot(solve_ref[:, 2 * rank : 4 * rank], jnp.concatenate([sums, sums], axis=0))
+        )
+        new_ref[rows, :] = turned.T.astype(BF16)
+        turned_ref[:, rows] = turned.astype(BF16)
+    store = pltpu.make_async_copy(new_ref, new_hbm, out_sem)
+    store.start()
     gram = dot(turned_ref[...], new_ref[...])
+    for copy in values:
+        copy.wait()
+    for pair in range(pairs):
+        genes = new_ref[2 * pair * blk : 2 * (pair + 1) * blk, :]
+        residual_pair(vals_ref, pos_ref, resid_ref, dot(cell_ref[...], genes, NT), 2 * pair, gene_blocks, 2 * pair)
+    total_ref[...] = dot(resid_ref[...], new_ref[...])
     owners, out_height, _ = out_ref.shape
     count = total_ref.shape[0] // owners
     lines = out_height - count
     for i in range(owners):
         out_ref[i, :count, :] = total_ref[i * count : (i + 1) * count, :].astype(BF16)
         out_ref[i, count:, :] = gram[i * lines : (i + 1) * lines, :].astype(BF16)
-    for store in stores:
-        store.wait()
+    store.wait()
 
 
 def second_pass(scale, owners, ids, count, values, cells, genes, sums):
@@ -374,7 +362,7 @@
         out_specs=(HBM, VMEM),
         scratch_shapes=[
             pltpu.SemaphoreType.DMA((PIECES + 3,)),
-            pltpu.SemaphoreType.DMA((len(SECOND_STAGES),)),
+            pltpu.SemaphoreType.DMA,
             pltpu.SMEM((slots,), jnp.int32),
             pltpu.SMEM((rows // blk * gene_blocks,), jnp.int32),
             pltpu.VMEM((slots + 1, blk, blk), BF16),
@@ -394,10 +382,9 @@
 def new_cells_kernel(scale, share, cell_ref, sums_ref, out_ref, solve_ref, gram_ref, inverse_ref):
     rank = cell_ref.shape[1]
     senders, height, _ = sums_ref.shape
-    half = (height - share) // 2
+    lines = height - share
     for i in range(senders):
-        gram = sums_ref[i, share:, :].astype(F32)
-        gram_ref[i * half : (i + 1) * half, :] = gram[:half, :] + gram[half:, :]
+        gram_ref[i * lines : (i + 1) * lines, :] = sums_ref[i, share:, :].astype(F32)
     solve_into(solve_ref, inverse_ref, gram_ref[...])
     sums = (sums_ref[:, :share, :].reshape(senders * share, rank).astype(F32) * (1.0 / scale)).astype(BF16)
     out_ref[...] = (
@@ -451,7 +438,7 @@
 
     sums = across_cells(first_pass(scale, ids, count, values, cell_factor, gene_factor))
     new_genes, cell_terms = second_pass(scale, n_gene, ids, count, values, cell_factor, gene_factor, sums)
-    cell_sums = exchange(add_cells(cell_share, exchange(cell_terms, "gene")), "gene")
+    cell_sums = exchange(add_cells(exchange(cell_terms, "gene")), "gene")
     new_cells = make_new_cells(scale, cell_share, cell_factor, cell_sums)
     return new_cells, new_genes
 

time: 136 us -> 135 us (level)
  no operation moved by 1% of the time
where the time goes in v5:
time: 135 us; the launch traced here: 134 us
  blocking collectives  97.6 us (72%)
  Pallas kernels  35.4 us (26%)
    all_to_all x6, blocking collectives, exchange(): lax.all_to_all(parts, axis, 0, 0, tiled=True, axis_index_groups=groups)  97.6 us
    pallas_call x1, Pallas kernels, second_pass(): pl.pallas_call(functools.partial(second_pass_kernel, scale), out_shape=(j...  17.1 us
    pallas_call x1, Pallas kernels, make_new_cells(): pl.pallas_call(functools.partial(new_cells_kernel, scale, share), out_sha...  12.8 us
    pallas_call x1, Pallas kernels, first_pass(): pl.pallas_call(functools.partial(first_pass_kernel, scale, gene_blocks),...  5.08 us

profile of v5, /device:TPU:1, one launch (start us, length us, event | category | flops | bytes accessed | tf_op | source)
XLA Modules:
  0.0 134.3 jit_solution(14155150441022352375)
XLA Ops:
  1.3 5.1 %first_pass.1 = bf16[32,128,128]{2,1,0:T(8,128)(2,1)} custom-call(s32[96]{0:T(128)} %bitcast.17, s32[1]{0:T(128)} %bitcast.8.count_ref, bf16[96,128,128]{2,1,0:T(8,128)(2,1)} %bitcast.10, bf16[512,128]{1,0:T(8,128)(2,1)} %cell_ref.1, bf16[3840,128]{1,0:T(8,128)(2,1)} %gene_hbm.3), custom_call_target="tpu_custom_call" | custom-call | tf_op jit(solution)/shard_map/first_pass/pallas_call | solution.py:142
  6.4 14.6 %all_to_all.30 = bf16[32,128,128]{2,1,0:T(8,128)(2,1)S(1)} all-to-all(bf16[32,128,128]{2,1,0:T(8,128)(2,1)} %first_pass.1), channel_id=1, replica_groups={{0,16,32,48},{64,80,96,112},{128,144,160,176},{192,208,224,240},{256,27..., dimensions={0} | all-to-all | bytes 2097152 | tf_op jit(solution)/shard_map/all_to_all | solution.py:416
  21.0 0.0 copy-start
  21.0 0.0 copy-start.1
  21.0 0.0 copy-start.2
  21.0 0.0 copy-start.3
  21.0 0.1 add_blocks.2
  21.1 23.9 %all_to_all.31 = bf16[8,128,128]{2,1,0:T(8,128)(2,1)S(1)} all-to-all(bf16[8,128,128]{2,1,0:T(8,128)(2,1)S(1)} %bitcast.14), channel_id=1, replica_groups={{0,64,128,192,256,320,384,448},{16,80,144,208,272,336,400,464},{32,96,1..., dimensions={0} | all-to-all | bytes 524288 | tf_op jit(solution)/shard_map/all_to_all | solution.py:416
  45.0 0.1 add_blocks.3
  45.0 11.8 %all_to_all.32.part_ref = bf16[8,128,128]{2,1,0:T(8,128)(2,1)S(1)} all-to-all(bf16[8,128,128]{2,1,0:T(8,128)(2,1)S(1)} %bitcast.16), channel_id=1, replica_groups={{0,64,128,192,256,320,384,448},{16,80,144,208,272,336,400,464},{32,96,1..., dimensions={0} | all-to-all | bytes 524288 | tf_op jit(solution)/shard_map/all_to_all | solution.py:416
  56.9 0.1 repeat.1
  57.0 13.0 %all_to_all.33.sums_ref = bf16[32,128,128]{2,1,0:T(8,128)(2,1)S(1)} all-to-all(bf16[32,128,128]{2,1,0:T(8,128)(2,1)S(1)} %bitcast.13), channel_id=1, replica_groups={{0,16,32,48},{64,80,96,112},{128,144,160,176},{192,208,224,240},{256,27..., dimensions={0} | all-to-all | bytes 2097152 | tf_op jit(solution)/shard_map/all_to_all | solution.py:416
  70.0 0.0 copy-done
  70.0 0.0 copy-done.1
  70.0 0.0 copy-done.2
  70.0 0.0 copy-done.3
  70.0 17.1 %second_pass.1 = (bf16[3840,128]{1,0:T(8,128)(2,1)}, bf16[16,40,128]{2,1,0:T(8,128)(2,1)S(1)}) custom-call(s32[96]{0:T(128)S(1)} %bitcast.18, s32[1]{0:T(128)} %bitcast.9.count_ref, bf16[96,128,128]{2,1,0:T(8,128)(2,1)S(1)} %bitcast.11, bf16[512,128]{1,0:T(8,128)(2,1)S(1)} %copy-done.2, bf16[3840,128]{1,0:T(8,128)(2,1)S(1)} %copy-done.1, ...), custom_call_target="tpu_custom_call" | custom-call | tf_op jit(solution)/shard_map/second_pass/pallas_call | solution.py:358
  87.1 22.0 %all_to_all.34.parts_ref = bf16[16,40,128]{2,1,0:T(8,128)(2,1)S(1)} all-to-all(bf16[16,40,128]{2,1,0:T(8,128)(2,1)S(1)} %get-tuple-element.4), channel_id=1, replica_groups=mesh['cell'=32,'gene'=16] {'gene'}, dimensions={0} | all-to-all | bytes 327680 | tf_op jit(solution)/shard_map/all_to_all | solution.py:416
  109.2 12.3 %all_to_all.35.sums_ref = bf16[16,40,128]{2,1,0:T(8,128)(2,1)S(1)} all-to-all(bf16[16,40,128]{2,1,0:T(8,128)(2,1)S(1)} %add_cells.1), channel_id=1, replica_groups=mesh['cell'=32,'gene'=16] {'gene'}, dimensions={0} | all-to-all | bytes 327680 | tf_op jit(solution)/shard_map/all_to_all | solution.py:416
  121.5 12.8 %new_cells.1 = bf16[512,128]{1,0:T(8,128)(2,1)} custom-call(bf16[512,128]{1,0:T(8,128)(2,1)S(1)} %copy-done.2, bf16[16,40,128]{2,1,0:T(8,128)(2,1)S(1)} %all_to_all.35.sums_ref), custom_call_target="tpu_custom_call" | custom-call | tf_op jit(solution)/shard_map/new_cells/pallas_call | solution.py:400
  (1 shorter events, 0.0 us)
Async XLA Ops:
  21.0 49.0 %copy-start = (bf16[1,1,96,128,128]{4,3,2,1,0:T(8,128)(2,1)S(1)}, bf16[1,1,96,128,128]{4,3,2,1,0:T(8,128)(2,1)}, u32[]{:S(2)}) copy-start(bf16[1,1,96,128,128]{4,3,2,1,0:T(8,128)(2,1)} %param.5) | copy-start | bytes 9437188
  21.0 49.0 %copy-start.1 = (bf16[3840,128]{1,0:T(8,128)(2,1)S(1)}, bf16[3840,128]{1,0:T(8,128)(2,1)}, u32[]{:S(2)}) copy-start(bf16[3840,128]{1,0:T(8,128)(2,1)} %gene_hbm.3) | copy-start | bytes 2949124
  21.0 49.0 %copy-start.2 = (bf16[512,128]{1,0:T(8,128)(2,1)S(1)}, bf16[512,128]{1,0:T(8,128)(2,1)}, u32[]{:S(2)}) copy-start(bf16[512,128]{1,0:T(8,128)(2,1)} %cell_ref.1) | copy-start | bytes 393220
  21.0 49.0 %copy-start.3 = (s32[1,1,96]{2,1,0:T(1,128)S(1)}, s32[1,1,96]{2,1,0:T(1,128)}, u32[]{:S(2)}) copy-start(s32[1,1,96]{2,1,0:T(1,128)} %param.6) | copy-start | bytes 1156

commit v6 on v5

--- a/solution.py
+++ b/solution.py
@@ -19,7 +19,7 @@
 FIRST_STAGES = (5, 10, 15)
 AHEAD = 8
 PIECES = 1
-INNER = 4
+INNER = 8
 
 
 def dot(a, b, dims=NN):

time: 135 us -> 132 us (0.978)
  blocking collectives: 97.6 us -> 95.3 us
    all_to_all x6, blocking collectives: 97.6 us -> 95.3 us  [exchange(): lax.all_to_all(parts, axis, 0, 0, tiled=True, axis_index_groups=groups)]
where the time goes in v6:
time: 132 us
  blocking collectives  95.3 us (72%)
  Pallas kernels  35.3 us (27%)
  between operations  1.33 us (1%)
    all_to_all x6, blocking collectives, exchange(): lax.all_to_all(parts, axis, 0, 0, tiled=True, axis_index_groups=groups)  95.3 us
    pallas_call x1, Pallas kernels, second_pass(): pl.pallas_call(functools.partial(second_pass_kernel, scale), out_shape=(j...  17.1 us
    pallas_call x1, Pallas kernels, make_new_cells(): pl.pallas_call(functools.partial(new_cells_kernel, scale, share), out_sha...  12.8 us
    pallas_call x1, Pallas kernels, first_pass(): pl.pallas_call(functools.partial(first_pass_kernel, scale, gene_blocks),...  5.08 us

profile of v6, /device:TPU:1, one launch (start us, length us, event | category | flops | bytes accessed | tf_op | source)
XLA Modules:
  0.0 132.0 jit_solution(1920734973354859938)
XLA Ops:
  1.3 5.1 %first_pass.1 = bf16[32,128,128]{2,1,0:T(8,128)(2,1)} custom-call(s32[96]{0:T(128)} %bitcast.17, s32[1]{0:T(128)} %bitcast.8.count_ref, bf16[96,128,128]{2,1,0:T(8,128)(2,1)} %bitcast.10, bf16[512,128]{1,0:T(8,128)(2,1)} %cell_ref.1, bf16[3840,128]{1,0:T(8,128)(2,1)} %gene_hbm.3), custom_call_target="tpu_custom_call" | custom-call | tf_op jit(solution)/shard_map/first_pass/pallas_call | solution.py:142
  6.4 18.2 %all_to_all.30 = bf16[32,128,128]{2,1,0:T(8,128)(2,1)S(1)} all-to-all(bf16[32,128,128]{2,1,0:T(8,128)(2,1)} %first_pass.1), channel_id=1, replica_groups={{0,16,32,48,64,80,96,112},{128,144,160,176,192,208,224,240},{256,272,28..., dimensions={0} | all-to-all | bytes 2097152 | tf_op jit(solution)/shard_map/all_to_all | solution.py:416
  24.5 0.0 copy-start
  24.5 0.0 copy-start.1
  24.5 0.0 copy-start.2
  24.5 0.0 copy-start.3
  24.5 0.1 add_blocks.2
  24.7 19.2 %all_to_all.31 = bf16[4,128,128]{2,1,0:T(8,128)(2,1)S(1)} all-to-all(bf16[4,128,128]{2,1,0:T(8,128)(2,1)S(1)} %bitcast.14), channel_id=1, replica_groups={{0,128,256,384},{16,144,272,400},{32,160,288,416},{48,176,304,432},{64,..., dimensions={0} | all-to-all | bytes 262144 | tf_op jit(solution)/shard_map/all_to_all | solution.py:416
  44.0 9.7 %all_to_all.32.part_ref = bf16[4,128,128]{2,1,0:T(8,128)(2,1)S(1)} all-to-all(bf16[4,128,128]{2,1,0:T(8,128)(2,1)S(1)} %bitcast.16), channel_id=1, replica_groups={{0,128,256,384},{16,144,272,400},{32,160,288,416},{48,176,304,432},{64,..., dimensions={0} | all-to-all | bytes 262144 | tf_op jit(solution)/shard_map/all_to_all | solution.py:416
  53.7 0.1 repeat.1
  53.8 13.1 %all_to_all.33.sums_ref = bf16[32,128,128]{2,1,0:T(8,128)(2,1)S(1)} all-to-all(bf16[32,128,128]{2,1,0:T(8,128)(2,1)S(1)} %bitcast.13), channel_id=1, replica_groups={{0,16,32,48,64,80,96,112},{128,144,160,176,192,208,224,240},{256,272,28..., dimensions={0} | all-to-all | bytes 2097152 | tf_op jit(solution)/shard_map/all_to_all | solution.py:416
  66.9 0.0 copy-done
  66.9 0.0 copy-done.1
  66.9 0.0 copy-done.2
  66.9 0.0 copy-done.3
  66.9 17.1 %second_pass.1 = (bf16[3840,128]{1,0:T(8,128)(2,1)}, bf16[16,40,128]{2,1,0:T(8,128)(2,1)S(1)}) custom-call(s32[96]{0:T(128)S(1)} %bitcast.18, s32[1]{0:T(128)} %bitcast.9.count_ref, bf16[96,128,128]{2,1,0:T(8,128)(2,1)S(1)} %bitcast.11, bf16[512,128]{1,0:T(8,128)(2,1)S(1)} %copy-done.2, bf16[3840,128]{1,0:T(8,128)(2,1)S(1)} %copy-done.1, ...), custom_call_target="tpu_custom_call" | custom-call | tf_op jit(solution)/shard_map/second_pass/pallas_call | solution.py:358
  84.0 22.8 %all_to_all.34.parts_ref = bf16[16,40,128]{2,1,0:T(8,128)(2,1)S(1)} all-to-all(bf16[16,40,128]{2,1,0:T(8,128)(2,1)S(1)} %get-tuple-element.4), channel_id=1, replica_groups=mesh['cell'=32,'gene'=16] {'gene'}, dimensions={0} | all-to-all | bytes 327680 | tf_op jit(solution)/shard_map/all_to_all | solution.py:416
  106.9 12.3 %all_to_all.35.sums_ref = bf16[16,40,128]{2,1,0:T(8,128)(2,1)S(1)} all-to-all(bf16[16,40,128]{2,1,0:T(8,128)(2,1)S(1)} %add_cells.1), channel_id=1, replica_groups=mesh['cell'=32,'gene'=16] {'gene'}, dimensions={0} | all-to-all | bytes 327680 | tf_op jit(solution)/shard_map/all_to_all | solution.py:416
  119.2 12.8 %new_cells.1 = bf16[512,128]{1,0:T(8,128)(2,1)} custom-call(bf16[512,128]{1,0:T(8,128)(2,1)S(1)} %copy-done.2, bf16[16,40,128]{2,1,0:T(8,128)(2,1)S(1)} %all_to_all.35.sums_ref), custom_call_target="tpu_custom_call" | custom-call | tf_op jit(solution)/shard_map/new_cells/pallas_call | solution.py:400
  (2 shorter events, 0.1 us)
Async XLA Ops:
  24.5 42.4 %copy-start = (bf16[1,1,96,128,128]{4,3,2,1,0:T(8,128)(2,1)S(1)}, bf16[1,1,96,128,128]{4,3,2,1,0:T(8,128)(2,1)}, u32[]{:S(2)}) copy-start(bf16[1,1,96,128,128]{4,3,2,1,0:T(8,128)(2,1)} %param.5) | copy-start | bytes 9437188
  24.5 42.4 %copy-start.1 = (bf16[3840,128]{1,0:T(8,128)(2,1)S(1)}, bf16[3840,128]{1,0:T(8,128)(2,1)}, u32[]{:S(2)}) copy-start(bf16[3840,128]{1,0:T(8,128)(2,1)} %gene_hbm.3) | copy-start | bytes 2949124
  24.5 42.4 %copy-start.2 = (bf16[512,128]{1,0:T(8,128)(2,1)S(1)}, bf16[512,128]{1,0:T(8,128)(2,1)}, u32[]{:S(2)}) copy-start(bf16[512,128]{1,0:T(8,128)(2,1)} %cell_ref.1) | copy-start | bytes 393220
  24.5 42.4 %copy-start.3 = (s32[1,1,96]{2,1,0:T(1,128)S(1)}, s32[1,1,96]{2,1,0:T(1,128)}, u32[]{:S(2)}) copy-start(s32[1,1,96]{2,1,0:T(1,128)} %param.6) | copy-start | bytes 1156

commit v7 on v6

--- a/solution.py
+++ b/solution.py
@@ -33,6 +33,10 @@
 def split(value):
     high = value.astype(BF16)
     return high, (value - high.astype(F32)).astype(BF16)
+
+
+def split_dot(a, b):
+    return dot(a[0], b[0]) + (dot(a[0], b[1]) + dot(a[1], b[0]))
 
 
 def two_terms(value):
@@ -266,7 +270,7 @@
     guess = (eye + (eye - matrix * across)) * down
     guess = guess + dot(guess.astype(BF16), dot(off, off).astype(BF16))
     rest = eye - exact_dot(matrix, guess)
-    inverse_ref[...] = guess + exact_dot(guess, rest)
+    inverse_ref[...] = guess + split_dot(split(guess), split(rest))
     size = jnp.sum(rest * rest)
 
     @pl.when(jnp.logical_not(size < 4e-6))
@@ -274,10 +278,10 @@
         inverse_ref[...] = eliminate(matrix, row, column)
 
     inverse = inverse_ref[...]
-    high, low = split(exact_dot(inverse, gram))
-    solve_ref[:, 0:rank] = high
-    solve_ref[:, rank : 2 * rank] = low
     high, low = split(inverse)
+    first, second = split(split_dot((high, low), split(gram)))
+    solve_ref[:, 0:rank] = first
+    solve_ref[:, rank : 2 * rank] = second
     solve_ref[:, 2 * rank : 3 * rank] = high
     solve_ref[:, 3 * rank : 4 * rank] = low
 

time: 132 us -> 132 us (level)
  no operation moved by 1% of the time
where the time goes in v7:
time: 132 us
  blocking collectives  95.3 us (72%)
  Pallas kernels  35 us (27%)
  between operations  1.33 us (1%)
    all_to_all x6, blocking collectives, exchange(): lax.all_to_all(parts, axis, 0, 0, tiled=True, axis_index_groups=groups)  95.3 us
    pallas_call x1, Pallas kernels, second_pass(): pl.pallas_call(functools.partial(second_pass_kernel, scale), out_shape=(j...  17 us
    pallas_call x1, Pallas kernels, make_new_cells(): pl.pallas_call(functools.partial(new_cells_kernel, scale, share), out_sha...  12.6 us
    pallas_call x1, Pallas kernels, first_pass(): pl.pallas_call(functools.partial(first_pass_kernel, scale, gene_blocks),...  5.08 us

profile of v7, /device:TPU:1, one launch (start us, length us, event | category | flops | bytes accessed | tf_op | source)
XLA Modules:
  0.0 131.7 jit_solution(4839420134031157396)
XLA Ops:
  1.3 5.1 %first_pass.1 = bf16[32,128,128]{2,1,0:T(8,128)(2,1)} custom-call(s32[96]{0:T(128)} %bitcast.17, s32[1]{0:T(128)} %bitcast.8.count_ref, bf16[96,128,128]{2,1,0:T(8,128)(2,1)} %bitcast.10, bf16[512,128]{1,0:T(8,128)(2,1)} %cell_ref.1, bf16[3840,128]{1,0:T(8,128)(2,1)} %gene_hbm.3), custom_call_target="tpu_custom_call" | custom-call | tf_op jit(solution)/shard_map/first_pass/pallas_call | solution.py:146
  6.4 18.2 %all_to_all.30 = bf16[32,128,128]{2,1,0:T(8,128)(2,1)S(1)} all-to-all(bf16[32,128,128]{2,1,0:T(8,128)(2,1)} %first_pass.1), channel_id=1, replica_groups={{0,16,32,48,64,80,96,112},{128,144,160,176,192,208,224,240},{256,272,28..., dimensions={0} | all-to-all | bytes 2097152 | tf_op jit(solution)/shard_map/all_to_all | solution.py:420
  24.5 0.0 copy-start
  24.5 0.0 copy-start.1
  24.5 0.0 copy-start.2
  24.5 0.0 copy-start.3
  24.5 0.1 add_blocks.2
  24.7 19.2 %all_to_all.31 = bf16[4,128,128]{2,1,0:T(8,128)(2,1)S(1)} all-to-all(bf16[4,128,128]{2,1,0:T(8,128)(2,1)S(1)} %bitcast.14), channel_id=1, replica_groups={{0,128,256,384},{16,144,272,400},{32,160,288,416},{48,176,304,432},{64,..., dimensions={0} | all-to-all | bytes 262144 | tf_op jit(solution)/shard_map/all_to_all | solution.py:420
  44.0 9.7 %all_to_all.32.part_ref = bf16[4,128,128]{2,1,0:T(8,128)(2,1)S(1)} all-to-all(bf16[4,128,128]{2,1,0:T(8,128)(2,1)S(1)} %bitcast.16), channel_id=1, replica_groups={{0,128,256,384},{16,144,272,400},{32,160,288,416},{48,176,304,432},{64,..., dimensions={0} | all-to-all | bytes 262144 | tf_op jit(solution)/shard_map/all_to_all | solution.py:420
  53.7 0.1 repeat.1
  53.8 13.1 %all_to_all.33.sums_ref = bf16[32,128,128]{2,1,0:T(8,128)(2,1)S(1)} all-to-all(bf16[32,128,128]{2,1,0:T(8,128)(2,1)S(1)} %bitcast.13), channel_id=1, replica_groups={{0,16,32,48,64,80,96,112},{128,144,160,176,192,208,224,240},{256,272,28..., dimensions={0} | all-to-all | bytes 2097152 | tf_op jit(solution)/shard_map/all_to_all | solution.py:420
  66.9 0.0 copy-done
  66.9 0.0 copy-done.1
  66.9 0.0 copy-done.2
  66.9 0.0 copy-done.3
  66.9 17.0 %second_pass.1 = (bf16[3840,128]{1,0:T(8,128)(2,1)}, bf16[16,40,128]{2,1,0:T(8,128)(2,1)S(1)}) custom-call(s32[96]{0:T(128)S(1)} %bitcast.18, s32[1]{0:T(128)} %bitcast.9.count_ref, bf16[96,128,128]{2,1,0:T(8,128)(2,1)S(1)} %bitcast.11, bf16[512,128]{1,0:T(8,128)(2,1)S(1)} %copy-done.2, bf16[3840,128]{1,0:T(8,128)(2,1)S(1)} %copy-done.1, ...), custom_call_target="tpu_custom_call" | custom-call | tf_op jit(solution)/shard_map/second_pass/pallas_call | solution.py:362
  83.9 22.8 %all_to_all.34.parts_ref = bf16[16,40,128]{2,1,0:T(8,128)(2,1)S(1)} all-to-all(bf16[16,40,128]{2,1,0:T(8,128)(2,1)S(1)} %get-tuple-element.4), channel_id=1, replica_groups=mesh['cell'=32,'gene'=16] {'gene'}, dimensions={0} | all-to-all | bytes 327680 | tf_op jit(solution)/shard_map/all_to_all | solution.py:420
  106.7 12.3 %all_to_all.35.sums_ref = bf16[16,40,128]{2,1,0:T(8,128)(2,1)S(1)} all-to-all(bf16[16,40,128]{2,1,0:T(8,128)(2,1)S(1)} %add_cells.1), channel_id=1, replica_groups=mesh['cell'=32,'gene'=16] {'gene'}, dimensions={0} | all-to-all | bytes 327680 | tf_op jit(solution)/shard_map/all_to_all | solution.py:420
  119.0 12.6 %new_cells.1 = bf16[512,128]{1,0:T(8,128)(2,1)} custom-call(bf16[512,128]{1,0:T(8,128)(2,1)S(1)} %copy-done.2, bf16[16,40,128]{2,1,0:T(8,128)(2,1)S(1)} %all_to_all.35.sums_ref), custom_call_target="tpu_custom_call" | custom-call | tf_op jit(solution)/shard_map/new_cells/pallas_call | solution.py:404
  (2 shorter events, 0.1 us)
Async XLA Ops:
  24.5 42.4 %copy-start = (bf16[1,1,96,128,128]{4,3,2,1,0:T(8,128)(2,1)S(1)}, bf16[1,1,96,128,128]{4,3,2,1,0:T(8,128)(2,1)}, u32[]{:S(2)}) copy-start(bf16[1,1,96,128,128]{4,3,2,1,0:T(8,128)(2,1)} %param.5) | copy-start | bytes 9437188
  24.5 42.4 %copy-start.1 = (bf16[3840,128]{1,0:T(8,128)(2,1)S(1)}, bf16[3840,128]{1,0:T(8,128)(2,1)}, u32[]{:S(2)}) copy-start(bf16[3840,128]{1,0:T(8,128)(2,1)} %gene_hbm.3) | copy-start | bytes 2949124
  24.5 42.4 %copy-start.2 = (bf16[512,128]{1,0:T(8,128)(2,1)S(1)}, bf16[512,128]{1,0:T(8,128)(2,1)}, u32[]{:S(2)}) copy-start(bf16[512,128]{1,0:T(8,128)(2,1)} %cell_ref.1) | copy-start | bytes 393220
  24.5 42.4 %copy-start.3 = (s32[1,1,96]{2,1,0:T(1,128)S(1)}, s32[1,1,96]{2,1,0:T(1,128)}, u32[]{:S(2)}) copy-start(s32[1,1,96]{2,1,0:T(1,128)} %param.6) | copy-start | bytes 1156

commit v8 on v7

--- a/solution.py
+++ b/solution.py
@@ -392,10 +392,8 @@
     solve_into(solve_ref, inverse_ref, gram_ref[...])
     sums = (sums_ref[:, :share, :].reshape(senders * share, rank).astype(F32) * (1.0 / scale)).astype(BF16)
     out_ref[...] = (
-        dot(cell_ref[...], solve_ref[:, 0:rank], NT)
-        + dot(cell_ref[...], solve_ref[:, rank : 2 * rank], NT)
-        + dot(sums, solve_ref[:, 2 * rank : 3 * rank], NT)
-        + dot(sums, solve_ref[:, 3 * rank : 4 * rank], NT)
+        dot(jnp.concatenate([cell_ref[...]] * 2, axis=1), solve_ref[:, 0 : 2 * rank], NT)
+        + dot(jnp.concatenate([sums] * 2, axis=1), solve_ref[:, 2 * rank : 4 * rank], NT)
     ).astype(BF16)
 
 

time: 132 us -> 132 us (level)
  no operation moved by 1% of the time
where the time goes in v8:
time: 132 us
  blocking collectives  95.3 us (72%)
  Pallas kernels  35 us (27%)
  between operations  1.33 us (1%)
    all_to_all x6, blocking collectives, exchange(): lax.all_to_all(parts, axis, 0, 0, tiled=True, axis_index_groups=groups)  95.3 us
    pallas_call x1, Pallas kernels, second_pass(): pl.pallas_call(functools.partial(second_pass_kernel, scale), out_shape=(j...  17 us
    pallas_call x1, Pallas kernels, make_new_cells(): pl.pallas_call(functools.partial(new_cells_kernel, scale, share), out_sha...  12.6 us
    pallas_call x1, Pallas kernels, first_pass(): pl.pallas_call(functools.partial(first_pass_kernel, scale, gene_blocks),...  5.08 us

profile of v8, /device:TPU:1, one launch (start us, length us, event | category | flops | bytes accessed | tf_op | source)
XLA Modules:
  0.0 131.7 jit_solution(4473670345576608603)
XLA Ops:
  1.3 5.1 %first_pass.1 = bf16[32,128,128]{2,1,0:T(8,128)(2,1)} custom-call(s32[96]{0:T(128)} %bitcast.17, s32[1]{0:T(128)} %bitcast.8.count_ref, bf16[96,128,128]{2,1,0:T(8,128)(2,1)} %bitcast.10, bf16[512,128]{1,0:T(8,128)(2,1)} %cell_ref.1, bf16[3840,128]{1,0:T(8,128)(2,1)} %gene_hbm.3), custom_call_target="tpu_custom_call" | custom-call | tf_op jit(solution)/shard_map/first_pass/pallas_call | solution.py:146
  6.4 18.2 %all_to_all.30 = bf16[32,128,128]{2,1,0:T(8,128)(2,1)S(1)} all-to-all(bf16[32,128,128]{2,1,0:T(8,128)(2,1)} %first_pass.1), channel_id=1, replica_groups={{0,16,32,48,64,80,96,112},{128,144,160,176,192,208,224,240},{256,272,28..., dimensions={0} | all-to-all | bytes 2097152 | tf_op jit(solution)/shard_map/all_to_all | solution.py:418
  24.5 0.0 copy-start
  24.5 0.0 copy-start.1
  24.5 0.0 copy-start.2
  24.5 0.0 copy-start.3
  24.5 0.1 add_blocks.2
  24.7 19.2 %all_to_all.31 = bf16[4,128,128]{2,1,0:T(8,128)(2,1)S(1)} all-to-all(bf16[4,128,128]{2,1,0:T(8,128)(2,1)S(1)} %bitcast.14), channel_id=1, replica_groups={{0,128,256,384},{16,144,272,400},{32,160,288,416},{48,176,304,432},{64,..., dimensions={0} | all-to-all | bytes 262144 | tf_op jit(solution)/shard_map/all_to_all | solution.py:418
  44.0 9.7 %all_to_all.32.part_ref = bf16[4,128,128]{2,1,0:T(8,128)(2,1)S(1)} all-to-all(bf16[4,128,128]{2,1,0:T(8,128)(2,1)S(1)} %bitcast.16), channel_id=1, replica_groups={{0,128,256,384},{16,144,272,400},{32,160,288,416},{48,176,304,432},{64,..., dimensions={0} | all-to-all | bytes 262144 | tf_op jit(solution)/shard_map/all_to_all | solution.py:418
  53.7 0.1 repeat.1
  53.8 13.1 %all_to_all.33.sums_ref = bf16[32,128,128]{2,1,0:T(8,128)(2,1)S(1)} all-to-all(bf16[32,128,128]{2,1,0:T(8,128)(2,1)S(1)} %bitcast.13), channel_id=1, replica_groups={{0,16,32,48,64,80,96,112},{128,144,160,176,192,208,224,240},{256,272,28..., dimensions={0} | all-to-all | bytes 2097152 | tf_op jit(solution)/shard_map/all_to_all | solution.py:418
  66.9 0.0 copy-done
  66.9 0.0 copy-done.1
  66.9 0.0 copy-done.2
  66.9 0.0 copy-done.3
  66.9 17.0 %second_pass.1 = (bf16[3840,128]{1,0:T(8,128)(2,1)}, bf16[16,40,128]{2,1,0:T(8,128)(2,1)S(1)}) custom-call(s32[96]{0:T(128)S(1)} %bitcast.18, s32[1]{0:T(128)} %bitcast.9.count_ref, bf16[96,128,128]{2,1,0:T(8,128)(2,1)S(1)} %bitcast.11, bf16[512,128]{1,0:T(8,128)(2,1)S(1)} %copy-done.2, bf16[3840,128]{1,0:T(8,128)(2,1)S(1)} %copy-done.1, ...), custom_call_target="tpu_custom_call" | custom-call | tf_op jit(solution)/shard_map/second_pass/pallas_call | solution.py:362
  83.9 22.8 %all_to_all.34.parts_ref = bf16[16,40,128]{2,1,0:T(8,128)(2,1)S(1)} all-to-all(bf16[16,40,128]{2,1,0:T(8,128)(2,1)S(1)} %get-tuple-element.4), channel_id=1, replica_groups=mesh['cell'=32,'gene'=16] {'gene'}, dimensions={0} | all-to-all | bytes 327680 | tf_op jit(solution)/shard_map/all_to_all | solution.py:418
  106.7 12.3 %all_to_all.35.sums_ref = bf16[16,40,128]{2,1,0:T(8,128)(2,1)S(1)} all-to-all(bf16[16,40,128]{2,1,0:T(8,128)(2,1)S(1)} %add_cells.1), channel_id=1, replica_groups=mesh['cell'=32,'gene'=16] {'gene'}, dimensions={0} | all-to-all | bytes 327680 | tf_op jit(solution)/shard_map/all_to_all | solution.py:418
  119.0 12.6 %new_cells.1 = bf16[512,128]{1,0:T(8,128)(2,1)} custom-call(bf16[512,128]{1,0:T(8,128)(2,1)S(1)} %copy-done.2, bf16[16,40,128]{2,1,0:T(8,128)(2,1)S(1)} %all_to_all.35.sums_ref), custom_call_target="tpu_custom_call" | custom-call | tf_op jit(solution)/shard_map/new_cells/pallas_call | solution.py:402
  (2 shorter events, 0.1 us)
Async XLA Ops:
  24.5 42.4 %copy-start = (bf16[1,1,96,128,128]{4,3,2,1,0:T(8,128)(2,1)S(1)}, bf16[1,1,96,128,128]{4,3,2,1,0:T(8,128)(2,1)}, u32[]{:S(2)}) copy-start(bf16[1,1,96,128,128]{4,3,2,1,0:T(8,128)(2,1)} %param.5) | copy-start | bytes 9437188
  24.5 42.4 %copy-start.1 = (bf16[3840,128]{1,0:T(8,128)(2,1)S(1)}, bf16[3840,128]{1,0:T(8,128)(2,1)}, u32[]{:S(2)}) copy-start(bf16[3840,128]{1,0:T(8,128)(2,1)} %gene_hbm.3) | copy-start | bytes 2949124
  24.5 42.4 %copy-start.2 = (bf16[512,128]{1,0:T(8,128)(2,1)S(1)}, bf16[512,128]{1,0:T(8,128)(2,1)}, u32[]{:S(2)}) copy-start(bf16[512,128]{1,0:T(8,128)(2,1)} %cell_ref.1) | copy-start | bytes 393220
  24.5 42.4 %copy-start.3 = (s32[1,1,96]{2,1,0:T(1,128)S(1)}, s32[1,1,96]{2,1,0:T(1,128)}, u32[]{:S(2)}) copy-start(s32[1,1,96]{2,1,0:T(1,128)} %param.6) | copy-start | bytes 1156

commit v9 on v7

--- a/solution.py
+++ b/solution.py
@@ -17,7 +17,7 @@
 VMEM = pl.BlockSpec(memory_space=pltpu.VMEM)
 HBM = pl.BlockSpec(memory_space=pltpu.HBM)
 FIRST_STAGES = (5, 10, 15)
-AHEAD = 8
+AHEAD = 6
 PIECES = 1
 INNER = 8
 

time: 132 us -> 132 us (level)
  no operation moved by 1% of the time
where the time goes in v9:
time: 132 us
  blocking collectives  95.3 us (72%)
  Pallas kernels  35.1 us (27%)
  between operations  1.33 us (1%)
    all_to_all x6, blocking collectives, exchange(): lax.all_to_all(parts, axis, 0, 0, tiled=True, axis_index_groups=groups)  95.3 us
    pallas_call x1, Pallas kernels, second_pass(): pl.pallas_call(functools.partial(second_pass_kernel, scale), out_shape=(j...  17 us
    pallas_call x1, Pallas kernels, make_new_cells(): pl.pallas_call(functools.partial(new_cells_kernel, scale, share), out_sha...  12.6 us
    pallas_call x1, Pallas kernels, first_pass(): pl.pallas_call(functools.partial(first_pass_kernel, scale, gene_blocks),...  5.15 us

profile of v9, /device:TPU:1, one launch (start us, length us, event | category | flops | bytes accessed | tf_op | source)
XLA Modules:
  0.0 131.7 jit_solution(481816032211527074)
XLA Ops:
  1.3 5.2 %first_pass.1 = bf16[32,128,128]{2,1,0:T(8,128)(2,1)} custom-call(s32[96]{0:T(128)} %bitcast.17, s32[1]{0:T(128)} %bitcast.8.count_ref, bf16[96,128,128]{2,1,0:T(8,128)(2,1)} %bitcast.10, bf16[512,128]{1,0:T(8,128)(2,1)} %cell_ref.1, bf16[3840,128]{1,0:T(8,128)(2,1)} %gene_hbm.3), custom_call_target="tpu_custom_call" | custom-call | tf_op jit(solution)/shard_map/first_pass/pallas_call | solution.py:146
  6.4 18.1 %all_to_all.30 = bf16[32,128,128]{2,1,0:T(8,128)(2,1)S(1)} all-to-all(bf16[32,128,128]{2,1,0:T(8,128)(2,1)} %first_pass.1), channel_id=1, replica_groups={{0,16,32,48,64,80,96,112},{128,144,160,176,192,208,224,240},{256,272,28..., dimensions={0} | all-to-all | bytes 2097152 | tf_op jit(solution)/shard_map/all_to_all | solution.py:420
  24.6 0.0 copy-start
  24.6 0.0 copy-start.1
  24.6 0.0 copy-start.2
  24.6 0.0 copy-start.3
  24.6 0.1 add_blocks.2
  24.7 19.3 %all_to_all.31 = bf16[4,128,128]{2,1,0:T(8,128)(2,1)S(1)} all-to-all(bf16[4,128,128]{2,1,0:T(8,128)(2,1)S(1)} %bitcast.14), channel_id=1, replica_groups={{0,128,256,384},{16,144,272,400},{32,160,288,416},{48,176,304,432},{64,..., dimensions={0} | all-to-all | bytes 262144 | tf_op jit(solution)/shard_map/all_to_all | solution.py:420
  44.0 9.7 %all_to_all.32.part_ref = bf16[4,128,128]{2,1,0:T(8,128)(2,1)S(1)} all-to-all(bf16[4,128,128]{2,1,0:T(8,128)(2,1)S(1)} %bitcast.16), channel_id=1, replica_groups={{0,128,256,384},{16,144,272,400},{32,160,288,416},{48,176,304,432},{64,..., dimensions={0} | all-to-all | bytes 262144 | tf_op jit(solution)/shard_map/all_to_all | solution.py:420
  53.7 0.1 repeat.1
  53.9 13.1 %all_to_all.33.sums_ref = bf16[32,128,128]{2,1,0:T(8,128)(2,1)S(1)} all-to-all(bf16[32,128,128]{2,1,0:T(8,128)(2,1)S(1)} %bitcast.13), channel_id=1, replica_groups={{0,16,32,48,64,80,96,112},{128,144,160,176,192,208,224,240},{256,272,28..., dimensions={0} | all-to-all | bytes 2097152 | tf_op jit(solution)/shard_map/all_to_all | solution.py:420
  67.0 0.0 copy-done
  67.0 0.0 copy-done.1
  67.0 0.0 copy-done.2
  67.0 0.0 copy-done.3
  67.0 17.0 %second_pass.1 = (bf16[3840,128]{1,0:T(8,128)(2,1)}, bf16[16,40,128]{2,1,0:T(8,128)(2,1)S(1)}) custom-call(s32[96]{0:T(128)S(1)} %bitcast.18, s32[1]{0:T(128)} %bitcast.9.count_ref, bf16[96,128,128]{2,1,0:T(8,128)(2,1)S(1)} %bitcast.11, bf16[512,128]{1,0:T(8,128)(2,1)S(1)} %copy-done.2, bf16[3840,128]{1,0:T(8,128)(2,1)S(1)} %copy-done.1, ...), custom_call_target="tpu_custom_call" | custom-call | tf_op jit(solution)/shard_map/second_pass/pallas_call | solution.py:362
  83.9 22.8 %all_to_all.34.parts_ref = bf16[16,40,128]{2,1,0:T(8,128)(2,1)S(1)} all-to-all(bf16[16,40,128]{2,1,0:T(8,128)(2,1)S(1)} %get-tuple-element.4), channel_id=1, replica_groups=mesh['cell'=32,'gene'=16] {'gene'}, dimensions={0} | all-to-all | bytes 327680 | tf_op jit(solution)/shard_map/all_to_all | solution.py:420
  106.8 12.3 %all_to_all.35.sums_ref = bf16[16,40,128]{2,1,0:T(8,128)(2,1)S(1)} all-to-all(bf16[16,40,128]{2,1,0:T(8,128)(2,1)S(1)} %add_cells.1), channel_id=1, replica_groups=mesh['cell'=32,'gene'=16] {'gene'}, dimensions={0} | all-to-all | bytes 327680 | tf_op jit(solution)/shard_map/all_to_all | solution.py:420
  119.1 12.6 %new_cells.1 = bf16[512,128]{1,0:T(8,128)(2,1)} custom-call(bf16[512,128]{1,0:T(8,128)(2,1)S(1)} %copy-done.2, bf16[16,40,128]{2,1,0:T(8,128)(2,1)S(1)} %all_to_all.35.sums_ref), custom_call_target="tpu_custom_call" | custom-call | tf_op jit(solution)/shard_map/new_cells/pallas_call | solution.py:404
  (2 shorter events, 0.1 us)
Async XLA Ops:
  24.6 42.4 %copy-start = (bf16[1,1,96,128,128]{4,3,2,1,0:T(8,128)(2,1)S(1)}, bf16[1,1,96,128,128]{4,3,2,1,0:T(8,128)(2,1)}, u32[]{:S(2)}) copy-start(bf16[1,1,96,128,128]{4,3,2,1,0:T(8,128)(2,1)} %param.5) | copy-start | bytes 9437188
  24.6 42.4 %copy-start.1 = (bf16[3840,128]{1,0:T(8,128)(2,1)S(1)}, bf16[3840,128]{1,0:T(8,128)(2,1)}, u32[]{:S(2)}) copy-start(bf16[3840,128]{1,0:T(8,128)(2,1)} %gene_hbm.3) | copy-start | bytes 2949124
  24.6 42.4 %copy-start.2 = (bf16[512,128]{1,0:T(8,128)(2,1)S(1)}, bf16[512,128]{1,0:T(8,128)(2,1)}, u32[]{:S(2)}) copy-start(bf16[512,128]{1,0:T(8,128)(2,1)} %cell_ref.1) | copy-start | bytes 393220
  24.6 42.4 %copy-start.3 = (s32[1,1,96]{2,1,0:T(1,128)S(1)}, s32[1,1,96]{2,1,0:T(1,128)}, u32[]{:S(2)}) copy-start(s32[1,1,96]{2,1,0:T(1,128)} %param.6) | copy-start | bytes 1156
